TPU v7x, 256 devices: a whole 4x4x8 slice. The times are simulated.
256 devices in a mesh: crop: 2 (over y_hi), dap: 128 (over y_lo, z, x, core).
Axes of the slice: x: 4, y: 4 (y_hi: 2, y_lo: 2; y = y_hi * 2 + y_lo), z: 8, core: 2. Of those that a mesh axis runs over, the one named last changes fastest.
Arguments:
- multiple_sequence_matrix: bfloat16 [128, 1024, 256], P('dap', 'crop'), parts along dimension 1, may hold values from -40 to 40
- layer_stretch: float32 [256], replicated, may hold values from 0.1 to 1.9
- layer_shift: float32 [256], replicated, may hold values from -3 to 3
- left_right_matrix: bfloat16 [256, 64], replicated, may hold values from -0.375 to 0.375
- mapping_offset: float32 [64], replicated, may hold values from -3 to 3
- final_projection_matrix: bfloat16 [1024, 128], replicated, may hold values from -2 to 2
- final_offset_vector: float32 [128], replicated, may hold values from -3 to 3
- couplet_adjoint: bfloat16 [512, 1024, 128], P('dap', 'crop'), parts along dimension 1, may hold values from -3 to 3
Outputs:
- pair_delta: bfloat16 [512, 1024, 128], P('dap', 'crop'), parts along dimension 1
- alignment_gradient: bfloat16 [128, 1024, 256], P('dap', 'crop'), parts along dimension 1
- proj_grad: float32 [512, 64], P('crop'), parts along dimension 0
- w_out_grad: float32 [2048, 128], P('crop'), parts along dimension 0
There are 2 independent parts, one for each index of `crop`. A program takes and returns all parts, laid end to end along the dimension named above; an argument that names none is the same for every part. Nothing has to cross between parts.
All inputs are finite; a program needn't handle non-finite values.
Results may differ from a plain program's by a relative error of at most 0.0069.
Values may be sent and summed in bfloat16 or wider, within the bound.
A program may use at most 64 MiB of HBM per device.

v0:
```python
import math

import jax
import jax.numpy as jnp
from jax import lax
from jax.sharding import PartitionSpec as P

EPSILON = 1e-05


def apply_norm(values, layer_stretch, layer_shift):
    entry_label = values.astype(jnp.float32)
    average = jnp.mean(entry_label, axis=-1, keepdims=True)
    centred = entry_label - average
    inverse_deviation = lax.rsqrt(jnp.mean(centred * centred, axis=-1, keepdims=True) + EPSILON)
    scaled_input = centred * inverse_deviation
    normed_input = (scaled_input * layer_stretch + layer_shift).astype(jnp.bfloat16)
    return (scaled_input, inverse_deviation, normed_input)


def project(normed_input, left_right_matrix, mapping_offset):
    flat = normed_input.reshape(-1, normed_input.shape[-1])
    result = jnp.dot(flat, left_right_matrix, preferred_element_type=jnp.float32) + mapping_offset
    return result.astype(jnp.bfloat16).reshape(
        normed_input.shape[:-1] + (left_right_matrix.shape[1],)
    )


def input_grads(
    projected_grad, normed_input, scaled_input, inverse_deviation, layer_stretch, left_right_matrix
):
    flat_grad = projected_grad.reshape(-1, projected_grad.shape[-1])
    weight_portion = lax.dot_general(
        normed_input.reshape(-1, normed_input.shape[-1]),
        flat_grad,
        (((0,), (0,)), ((), ())),
        preferred_element_type=jnp.float32,
    )
    normed_grad = lax.dot_general(
        flat_grad, left_right_matrix, (((1,), (1,)), ((), ())), preferred_element_type=jnp.float32
    ).reshape(normed_input.shape)
    hidden_width = normed_grad * layer_stretch
    alignment_gradient = inverse_deviation * (
        hidden_width
        - jnp.mean(hidden_width, axis=-1, keepdims=True)
        - scaled_input * jnp.mean(hidden_width * scaled_input, axis=-1, keepdims=True)
    )
    return (weight_portion, alignment_gradient.astype(jnp.bfloat16))


def pair_terms(
    left_rows, piece, grad_block, final_projection_matrix, final_offset_vector, row_count
):
    own_count, feature_depth, pair_width = grad_block.shape
    chan = piece.shape[1] // feature_depth
    product = lax.dot_general(
        left_rows, piece, (((0,), (0,)), ((), ())), preferred_element_type=jnp.float32
    )
    outer = (product / row_count).astype(jnp.bfloat16).reshape(own_count, chan, feature_depth, chan)
    outer = jnp.transpose(outer, (0, 2, 1, 3)).reshape(own_count * feature_depth, chan * chan)
    update = (
        jnp.dot(outer, final_projection_matrix, preferred_element_type=jnp.float32)
        + final_offset_vector
    ).astype(jnp.bfloat16)
    flat_grad = grad_block.reshape(-1, pair_width)
    outer_grad = lax.dot_general(
        flat_grad,
        final_projection_matrix,
        (((1,), (1,)), ((), ())),
        preferred_element_type=jnp.float32,
    ).astype(jnp.bfloat16)
    weight_term = lax.dot_general(
        outer, flat_grad, (((0,), (0,)), ((), ())), preferred_element_type=jnp.float32
    )
    regrouped = jnp.transpose(
        outer_grad.reshape(own_count, feature_depth, chan, chan), (0, 2, 1, 3)
    )
    regrouped = regrouped.reshape(own_count * chan, feature_depth * chan)
    left_term = lax.dot_general(
        piece, regrouped, (((1,), (1,)), ((), ())), preferred_element_type=jnp.float32
    )
    return (update.reshape(own_count, feature_depth, pair_width), weight_term, left_term, regrouped)


def shards(
    multiple_sequence_matrix,
    layer_stretch,
    layer_shift,
    left_right_matrix,
    mapping_offset,
    final_projection_matrix,
    final_offset_vector,
    couplet_adjoint,
):
    segment_collection = lax.axis_size("dap")
    homolog_slice, amino_position, feature_depth = multiple_sequence_matrix.shape
    amino_slice = couplet_adjoint.shape[0]
    pair_width = couplet_adjoint.shape[2]
    row_count = homolog_slice * segment_collection
    chan = left_right_matrix.shape[1] // 2
    moved_axes = lax.all_to_all(
        multiple_sequence_matrix.reshape(
            homolog_slice, segment_collection, amino_slice * feature_depth
        ),
        "dap",
        split_axis=1,
        concat_axis=0,
        tiled=True,
    )
    alignment_columns = moved_axes.reshape(row_count, amino_slice, feature_depth)
    scaled_input, inverse_deviation, normed_input = apply_norm(
        alignment_columns, layer_stretch, layer_shift
    )
    projected = project(normed_input, left_right_matrix, mapping_offset)
    left_rows = projected[:, :, :chan].reshape(row_count, amino_slice * chan)
    right_rows = projected[:, :, chan:].reshape(row_count, amino_slice * chan)
    update_init = jnp.zeros((amino_slice, amino_position, pair_width), jnp.bfloat16)
    weight_init = jnp.zeros((chan * chan, pair_width), jnp.float32)
    left_init = jnp.zeros((row_count, amino_slice * chan), jnp.float32)
    piece = lax.all_gather(right_rows, "dap", axis=1, tiled=True)
    count = piece.shape[1] // chan
    block = math.gcd(count, 128)

    def inner(number, state):
        update_holder, weight_sum, left_sum, column_buf = state
        offset = number * block
        part_right = lax.dynamic_slice_in_dim(piece, number * block * chan, block * chan, 1)
        part_grad = lax.dynamic_slice_in_dim(couplet_adjoint, offset, block, 1)
        update, weight_term, left_term, regrouped = pair_terms(
            left_rows,
            part_right,
            part_grad,
            final_projection_matrix,
            final_offset_vector,
            row_count,
        )
        right_term = jnp.dot(left_rows, regrouped, preferred_element_type=jnp.float32)
        update_holder = lax.dynamic_update_slice_in_dim(update_holder, update, offset, 1)
        column_buf = lax.dynamic_update_slice_in_dim(column_buf, right_term, offset * chan, 1)
        return (update_holder, weight_sum + weight_term, left_sum + left_term, column_buf)

    update_holder, weight_sum, left_sum, column_buf = lax.fori_loop(
        0,
        count // block,
        inner,
        (
            update_init,
            weight_init,
            left_init,
            jnp.zeros((row_count, amino_position * chan), jnp.float32),
        ),
    )
    right_sum = lax.psum_scatter(column_buf, "dap", scatter_dimension=1, tiled=True)
    left_grad = (left_sum / row_count).reshape(row_count, amino_slice, chan)
    right_grad = (right_sum / row_count).reshape(row_count, amino_slice, chan)
    projected_grad = jnp.concatenate([left_grad, right_grad], axis=-1).astype(jnp.bfloat16)
    weight_portion, grad_cols = input_grads(
        projected_grad,
        normed_input,
        scaled_input,
        inverse_deviation,
        layer_stretch,
        left_right_matrix,
    )
    backward_pass = lax.all_to_all(
        grad_cols.reshape(row_count, 1, amino_slice * feature_depth),
        "dap",
        split_axis=0,
        concat_axis=1,
        tiled=True,
    )
    alignment_gradient = backward_pass.reshape(homolog_slice, amino_position, feature_depth)
    projector_total, output_total = lax.psum((weight_portion, weight_sum), "dap")
    return (
        update_holder,
        alignment_gradient,
        projector_total / amino_position,
        output_total * (math.sqrt(row_count) / amino_position),
    )


def solution(mesh):
    placed = (P("dap", "crop", None), P(), P(), P(), P(), P(), P(), P("dap", "crop", None))
    return jax.shard_map(
        shards,
        mesh=mesh,
        in_specs=placed,
        out_specs=(
            P("dap", "crop", None),
            P("dap", "crop", None),
            P("crop", None),
            P("crop", None),
        ),
        check_vma=False,
    )
```

profile of v0, /device:TPU:1, one launch (start us, length us, event | category | flops | bytes accessed | tf_op | source)
XLA Modules:
  0.0 1956.6 jit_solution(487795506004908131)
XLA Ops:
  7.2 2.0 reshape.175
  9.8 2.1 reduce.1
  12.1 29.7 %all_to_all.8 = bf16[128,2,512]{2,1,0:T(2,128)(2,1)S(1)} all-to-all(bf16[128,2,512]{2,1,0:T(2,128)(2,1)S(1)} %reshape.177), channel_id=1, replica_groups=mesh['crop'=2,'dap'=128] {'dap'}, dimensions={0} | all-to-all | bytes 524288 | tf_op jit(solution)/shard_map/all_to_all | solution.py:101
  45.6 209.0 %all-gather.2.cloned.1.call-done = bf16[128,16384]{0,1:T(8,128)(2,1)} async-done(((bf16[128,128]{0,1:T(8,128)(2,1)}), bf16[128,16384]{0,1:T(8,128)(2,1)}) %all-gather.2.cloned.1.call-update) | async-done | bytes 4194320 | tf_op jit(solution)/shard_map/all_gather | solution.py:120
  254.7 0.9 broadcast_in_dim.11
  255.5 3.5 broadcast_in_dim.26
  259.0 107.7 %while.22 = (s32[]{:T(128)}, bf16[4,512,128]{2,1,0:T(8,128)(2,1)}, f32[1024,128]{1,0:T(8,128)S(1)}, f32[128,128]{1,0:T(8,128)S(1)}, f32[128,16384]{0,1:T(8,128)}...) while((s32[]{:T(128)}, bf16[4,512,128]{2,1,0:T(8,128)(2,1)}, ...), condition=%wide.region_3.0_spmd.clone, body=%wide.region_2.0_spmd.clone.sunk | while | flops 807305216 | bytes 27855664 | solution.py:142
  259.0 1.6 fusion.62
  261.2 4.5 reshape.184
  265.7 3.7 copy.87
  269.9 1.6 constant_dynamic-slice_fusion.2
  273.3 3.2 copy.89
  276.5 5.9 reshape.186
  282.4 1.7 convolution_add_fusion.7
  284.1 1.8 fusion.64
  286.0 1.6 fusion.62
  288.2 4.5 reshape.184
  292.6 3.7 copy.87
  296.8 1.6 constant_dynamic-slice_fusion.2
  300.3 3.2 copy.89
  303.5 5.9 reshape.186
  309.4 1.7 convolution_add_fusion.7
  311.1 1.8 fusion.64
  312.9 1.6 fusion.62
  315.0 4.5 reshape.184
  319.5 3.7 copy.87
  323.7 1.6 constant_dynamic-slice_fusion.2
  327.2 3.2 copy.89
  330.4 5.9 reshape.186
  336.2 1.7 convolution_add_fusion.7
  338.0 1.8 fusion.64
  339.8 1.6 fusion.62
  342.0 4.5 reshape.184
  346.5 3.7 copy.87
  350.6 1.6 constant_dynamic-slice_fusion.2
  354.1 3.2 copy.89
  357.3 5.9 reshape.186
  363.2 1.7 convolution_add_fusion.7
  364.9 1.8 fusion.64
  367.6 569.4 %reduce-scatter.2.cloned.1.call-done = f32[128,128]{0,1:T(8,128)} async-done(((f32[128,16384]{0,1:T(8,128)}), f32[128,128]{0,1:T(8,128)}) %reduce-scatter.2.cloned.1.call-update) | async-done | bytes 65552 | tf_op jit(solution)/shard_map/reduce_scatter | solution.py:153
  937.0 0.8 multiply_convert_fusion.1
  937.9 1.0 convolution_bitcast_fusion.1
  940.9 26.4 %all_to_all.9 = bf16[128,2,512]{2,1,0:T(2,128)(2,1)S(1)} all-to-all(bf16[128,2,512]{2,1,0:T(2,128)(2,1)S(1)} %reshape.179), channel_id=1, replica_groups=mesh['crop'=2,'dap'=128] {'dap'}, dimensions={0} | all-to-all | bytes 524288 | tf_op jit(solution)/shard_map/all_to_all | solution.py:165
  967.5 1.5 reduce
  969.0 0.9 reshape.164
  969.9 976.8 %all-reduce.3.cloned.1.call-done = (f32[256,64]{0,1:T(8,128)}, f32[1024,128]{1,0:T(8,128)}) async-done(((f32[256,64]{0,1:T(8,128)}, f32[1024,128]{1,0:T(8,128)}), (f32[256,64]{0,1:T(8,128)}, f32[1024,128]{1,0:T(8,128)})) %all-reduce.3.cloned.1.call-update) | async-done | bytes 589840 | tf_op jit(solution)/shard_map/psum | solution.py:173
  1946.7 1.5 broadcast_multiply_fusion.1
  1948.2 1.9 broadcast_multiply_fusion
  (84 shorter events, 19.0 us)
Async XLA Ops:
  7.2 36.6 %copy-start = (bf16[256,64]{0,1:T(8,128)(2,1)S(1)}, bf16[256,64]{0,1:T(8,128)(2,1)}, u32[]{:S(2)}) copy-start(bf16[256,64]{0,1:T(8,128)(2,1)} %param.13) | copy-start | bytes 98308
  7.2 247.5 %all-gather.2.cloned.1.call-start = ((), (), s32[]{:S(2)}) async-start(), calls=%async_computation.3 | async-start | bytes 4227072 | tf_op jit(solution)/shard_map/all_gather | solution.py:120
  9.7 34.0 %copy-start.3 = (f32[256]{0:T(256)S(1)}, f32[256]{0:T(256)}, u32[]{:S(2)}) copy-start(f32[256]{0:T(256)} %param.11) | copy-start | bytes 3076
  9.7 34.0 %copy-start.4 = (f32[256]{0:T(256)S(1)}, f32[256]{0:T(256)}, u32[]{:S(2)}) copy-start(f32[256]{0:T(256)} %param.12) | copy-start | bytes 3076
  9.8 34.0 %copy-start.5 = (f32[64]{0:T(128)S(1)}, f32[64]{0:T(128)}, u32[]{:S(2)}) copy-start(f32[64]{0:T(128)} %param.14) | copy-start | bytes 772
  45.2 891.9 %reduce-scatter.2.cloned.1.call-start = ((), (), s32[]{:S(2)}) async-start(), calls=%async_computation.4 | async-start | bytes 8454144 | tf_op jit(solution)/shard_map/reduce_scatter | solution.py:153
  255.5 3.5 copy-start.2
  261.2 8.2 copy-start.6
  288.1 8.2 copy-start.6
  315.0 8.2 copy-start.6
  342.0 8.2 copy-start.6
  366.7 0.8 copy-start.1
  367.5 1579.2 %all-reduce.3.cloned.1.call-start = ((), (), s32[]{:S(2)}) async-start(), calls=%async_computation.5 | async-start | bytes 1179648 | tf_op jit(solution)/shard_map/psum | solution.py:173
Sparse Core Ops, SparseCore 0:
  45.3 209.3 all-gather.1
  366.9 570.1 reduce-scatter.1
  940.5 1006.1 all-reduce.2
where the time goes:
time: 1960 us
  waiting for transfers between devices  1760 us (90%)
  local copies, waits for them, and re-layouts  93.1 us (5%)
  blocking collectives  56.1 us (3%)
  matrix products  28.3 us (1%)
    psum x1, waiting for transfers between devices, shards(): lax.psum((weight_portion, weight_sum), 'dap')  977 us
    reduce_scatter x1, waiting for transfers between devices, shards(): lax.psum_scatter(column_buf, 'dap', scatter_dimension=1, tiled=True)  569 us
    all_gather x1, waiting for transfers between devices, shards(): piece = lax.all_gather(right_rows, 'dap', axis=1, tiled=True)  209 us
  transfers between devices with their start and end apart: 3, of which 3 were waited for; matrix products, arithmetic and copies ran while one was open for 0% of the time, Pallas kernels for 0%

commit v1 on v0

v1 whole, which is shorter than its diff:
```python
import math

import jax
import jax.numpy as jnp
from jax import lax
from jax.experimental import pallas as pl
from jax.experimental.pallas import tpu as pltpu
from jax.sharding import PartitionSpec as P

EPSILON = 1e-05
MESH = pl.DeviceIdType.MESH
f32 = jnp.float32
bf16 = jnp.bfloat16

NX, NZ, NM = 4, 8, 16
CH = 32
ROWS = 128
RES = 512


def dot(a, b):
    return jnp.dot(a, b, preferred_element_type=f32)


def dot_nt(a, b):
    return lax.dot_general(a, b, (((1,), (1,)), ((), ())), preferred_element_type=f32)


def loop(low, high, body):
    def step(k, carry):
        body(k)
        return carry

    lax.fori_loop(low, high, step, 0)


def kernel(
    msa, stretch, shift, wlr, offs, wf, fbias, adj,
    pd_out, ag_out, pg_out, wo_out,
    scaled, inv, nf, nb, np_, wl4t, wrt, lrow, rt,
    sb, rb, rbf, ls, rs, lmat, lt, rmat, amat, wff, w2, w2t,
    gmat, xmat, rgs, rgr, rgo, rz, rzr, lacc, lgs, lzr, bsf, bs, br, ng,
    wpart, wsend, wrecv, wzs, wzr, wzg, wfin, pdb,
    psend, precv, pzs, pzr, pgs, pgr,
    s1s, s1r, cps, cpr, zls, zlr, zrs, zrr, crs, crr, rgss, rgrs, bzs, bzr, bls, blr, b1s, b1r,
    pds, pdr, w1s, w1r, wzss, wzrs, wgs, wgr, was, war, p1s, p1r, pzss, pzrs, pas, par,
):
    me = lax.axis_index("dap")
    core = lax.rem(me, 2)
    x = lax.rem(me // 2, NX)
    z = lax.rem(me // 8, NZ)
    y = me // 64
    m = y * 8 + x * 2 + core
    other = 1 - core

    def plane_dev(mm):
        return (mm // 8) * 64 + z * 8 + lax.rem(mm, 8)

    def z_dev(zz):
        return y * 64 + zz * 8 + x * 2 + core

    def x_dev(xx):
        return y * 64 + z * 8 + xx * 2 + core

    core_dev = y * 64 + z * 8 + x * 2 + other

    def rcopy(src, dst, ss, rs_, dev):
        return pltpu.make_async_remote_copy(
            src_ref=src, dst_ref=dst, send_sem=ss, recv_sem=rs_, device_id={"dap": dev}, device_id_type=MESH
        )

    def planes(body):
        loop(1, NM, lambda k: body(lax.rem(m + k, NM)))

    def zs(body):
        loop(1, NZ, lambda k: body(lax.rem(z + k, NZ)))

    def xs(body):
        loop(1, NX, lambda k: body(lax.rem(x + k, NX)))

    barrier = pltpu.get_barrier_semaphore()
    planes(lambda mm: pl.semaphore_signal(barrier, inc=1, device_id={"dap": plane_dev(mm)}, device_id_type=MESH))
    zs(lambda zz: pl.semaphore_signal(barrier, inc=1, device_id={"dap": z_dev(zz)}, device_id_type=MESH))

    def norm_rows(k):
        rows = pl.ds(pl.multiple_of(k * 64, 64), 64)
        v = msa[0, rows, :].astype(f32)
        c = v - jnp.mean(v, axis=-1, keepdims=True)
        iv = lax.rsqrt(jnp.mean(c * c, axis=-1, keepdims=True) + EPSILON)
        sc = c * iv
        scaled[rows, :] = sc
        inv[rows, :] = jnp.broadcast_to(iv, (64, 128))
        n = (sc * stretch[...] + shift[...]).astype(bf16)
        nb[rows, :] = n
        n = n.astype(f32)
        nf[0, rows, :] = n[:, :128]
        nf[1, rows, :] = n[:, 128:]

    loop(0, 8, norm_rows)
    for r in range(4):
        for yc in range(4):
            start = (yc // 2) * 256 + (yc % 2) * 4 + r
            for h in range(2):
                np_[pl.ds(r * 128 + yc * 32, 32), pl.ds(h * 128, 128)] = nf[
                    h, pl.ds(start, 32, stride=8), :
                ].astype(bf16)

    w_rows = wlr[...]
    wlrt = w_rows.astype(f32).T
    wrt[...] = wlrt[CH:, :].astype(bf16)
    spread = lax.broadcasted_iota(jnp.int32, (64, 128), 0) == (lax.broadcasted_iota(jnp.int32, (64, 128), 1) & 31)
    wl4 = dot(w_rows, spread.astype(f32).astype(bf16))
    wl4t[...] = wl4.T.astype(bf16)
    diag = lax.broadcasted_iota(jnp.int32, (64, 64), 0) == lax.broadcasted_iota(jnp.int32, (64, 64), 1)
    offs_col = jnp.sum(jnp.where(diag, jnp.broadcast_to(offs[...], (64, 64)), 0.0), axis=1, keepdims=True)
    offs4 = jnp.sum(jnp.where(spread, jnp.broadcast_to(offs_col, (64, 128)), 0.0), axis=0, keepdims=True)
    lane_r = lax.broadcasted_iota(jnp.int32, (256, 128), 1) >> 5
    left = jnp.zeros((128, 128), f32)
    for r in range(4):
        left = left + dot(np_[pl.ds(r * 128, 128), :], jnp.where(lane_r == r, wl4, 0.0).astype(bf16))
    lrow[...] = (left + offs4).astype(bf16)
    rt[...] = (dot_nt(wlrt[CH:, :].astype(bf16), nb[...]) + offs_col[CH:, :]).astype(bf16)
    for mm in range(NM):
        yc = (mm // 8) * 2 + mm % 2
        xx, cc = (mm % 8) // 2, mm % 2
        sb[mm, pl.ds(0, 32), :] = lrow[pl.ds(yc * 32, 32), :]
        sb[mm, pl.ds(32, 16), :] = rt[pl.ds(cc * 16, 16), pl.ds(xx * 128, 128)]

    pl.semaphore_wait(barrier, NM - 1 + NZ - 1)

    planes(lambda mm: rcopy(sb.at[mm], rb.at[m], s1s.at[mm], s1r.at[m], plane_dev(mm)).start())
    rb[m] = sb[m]

    def adj_part(xx):
        return adj.at[:, pl.ds(pl.multiple_of(xx * 128, 128), 128), :]

    def own_i(xx):
        return amat.at[pl.ds(xx * 4, 4)]

    xs(lambda xx: rcopy(adj_part(xx), own_i(x), cps.at[xx], cpr.at[x], x_dev(xx)).start())
    amat[pl.ds(x * 4, 4)] = adj[:, pl.ds(pl.multiple_of(x * 128, 128), 128), :]

    wff[...] = wf[...].astype(f32)
    for d in range(CH):
        w2[pl.ds(d * 32, 32), :] = wff[pl.ds(d, 32, stride=32), :].astype(bf16)
    for k in range(8):
        w2t[:, pl.ds(k * 128, 128)] = w2[pl.ds(k * 128, 128), :].astype(f32).T.astype(bf16)

    planes(lambda mm: rcopy(sb.at[mm], rb.at[mm], s1s.at[mm], s1r.at[mm], plane_dev(mm)).wait_recv())

    loop(0, NM, lambda k: rbf.__setitem__((pl.ds(pl.multiple_of(k * 48, 48), 48), slice(None)), rb[k].astype(f32)))
    for zz in range(NZ):
        for xx in range(NX):
            ls[zz, :, pl.ds(xx * 128, 128)] = rbf[pl.ds(zz * 4 + xx, 16, stride=48), :].astype(bf16)
    for d in range(16):
        rs[:, pl.ds(d * 128, 128)] = rbf[pl.ds(32 + d, 16, stride=48), :].astype(bf16)

    def zrows(zz):
        return pl.ds(pl.multiple_of(zz * 16, 16), 16)

    def half(cc):
        return pl.ds(pl.multiple_of(cc * 2048, 2048), 2048)

    zs(lambda zz: rcopy(ls.at[zz], lmat.at[zrows(z), :], zls.at[zz], zlr.at[z], z_dev(zz)).start())
    zs(lambda zz: rcopy(rs, rmat.at[zrows(z), half(core)], zrs.at[zz], zrr.at[z], z_dev(zz)).start())
    rcopy(rs, rmat.at[zrows(z), half(core)], crs.at[z], crr.at[z], core_dev).start()
    lmat[zrows(z), :] = ls[z]
    rmat[zrows(z), half(core)] = rs[...]

    def r_piece(zz, cc):
        return rmat.at[zrows(zz), half(cc)]

    xs(lambda xx: rcopy(adj_part(xx), own_i(xx), cps.at[xx], cpr.at[xx], x_dev(xx)).wait_recv())

    def grad_pair(t):
        a2 = amat[pl.ds(t * 2, 2)].reshape(256, 128)
        for q in range(4):
            g = dot_nt(w2[pl.ds(q * 256, 256), :], a2)
            for e in range(8):
                for u in range(2):
                    rows = pl.ds(pl.multiple_of((2 * t + u) * 32, 32), 32)
                    gmat[rows, pl.ds((q * 8 + e) * 128, 128)] = g[e * 32 : e * 32 + 32, u * 128 : u * 128 + 128].astype(
                        bf16
                    )

    loop(0, 8, grad_pair)

    def forward(zz):
        rcopy(rs, r_piece(zz, core), zrs.at[zz], zrr.at[zz], z_dev(zz)).wait_recv()
        rcopy(r_piece(zz, core), r_piece(zz, core), crs.at[zz], crr.at[zz], core_dev).start()

    zs(forward)

    zs(lambda zz: rcopy(ls.at[zz], lmat.at[zrows(zz), :], zls.at[zz], zlr.at[zz], z_dev(zz)).wait_recv())
    for k in range(4):
        lt[pl.ds(k * 128, 128), :] = lmat[:, pl.ds(k * 128, 128)].astype(f32).T.astype(bf16)

    def right_other(k):
        cols = pl.ds(pl.multiple_of(other * 2048 + k * 512, 512), 512)
        rgs[:, pl.ds(pl.multiple_of(k * 512, 512), 512)] = (dot(lmat[...], gmat[:, cols]) * (1.0 / ROWS)).astype(bf16)

    loop(0, 4, right_other)
    rg_copy = rcopy(rgs, rgr, rgss, rgrs, core_dev)
    rg_copy.start()

    def right_own(k):
        cols = pl.ds(pl.multiple_of(core * 2048 + k * 512, 512), 512)
        rgo[:, pl.ds(pl.multiple_of(k * 512, 512), 512)] = dot(lmat[...], gmat[:, cols]) * (1.0 / ROWS)

    loop(0, 4, right_own)
    rg_copy.wait_recv()

    def right_add(k):
        cols = pl.ds(pl.multiple_of(k * 512, 512), 512)
        rz[:, cols] = (rgo[:, cols] + rgr[:, cols].astype(f32)).astype(bf16)

    loop(0, 4, right_add)
    zs(lambda zz: rcopy(rz.at[zrows(zz), :], rzr.at[z], bzs.at[zz], bzr.at[z], z_dev(zz)).start())
    rzr[z] = rz[zrows(z), :]

    loop(0, NZ, lambda zz: rcopy(r_piece(zz, other), r_piece(zz, other), crs.at[zz], crr.at[zz], core_dev).wait_recv())
    lacc[...] = jnp.zeros((128, 512), f32)

    def left_part(k):
        cols = pl.ds(pl.multiple_of(k * 1024, 1024), 1024)
        lacc[...] += dot_nt(rmat[:, cols], gmat[:, cols])

    loop(0, 4, left_part)
    lgs[...] = (lacc[...] * (1.0 / ROWS)).astype(bf16)
    zs(lambda zz: rcopy(lgs.at[zrows(zz), :], lzr.at[z], bls.at[zz], blr.at[z], z_dev(zz)).start())
    lzr[z] = lgs[zrows(z), :]

    def outer_part(n):
        o = dot(lt[...], rmat[:, pl.ds(pl.multiple_of(n * 256, 256), 256)]) * (1.0 / ROWS)
        for i in range(16):
            for e in range(2):
                rows = pl.ds(pl.multiple_of((2 * n + e) * 32, 32), 32)
                xmat[rows, pl.ds(i * 128, 128)] = o[i * 32 : i * 32 + 32, e * 128 : e * 128 + 128].astype(bf16)

    loop(0, 16, outer_part)

    def delta_pair(t):
        p = dot(w2t[...], xmat[:, pl.ds(pl.multiple_of(t * 256, 256), 256)])
        pdb[pl.ds(t * 2, 2)] = (p.T + fbias[...]).astype(bf16).reshape(2, 128, 128)

    loop(0, 8, delta_pair)

    def out_part(xx):
        return pd_out.at[:, pl.ds(pl.multiple_of(xx * 128, 128), 128), :]

    xs(lambda xx: rcopy(pdb.at[pl.ds(xx * 4, 4)], out_part(x), pds.at[xx], pdr.at[x], x_dev(xx)).start())
    pd_out[:, pl.ds(pl.multiple_of(x * 128, 128), 128), :] = pdb[pl.ds(x * 4, 4)]

    def w_part(n):
        rows = pl.ds(pl.multiple_of(n * 256, 256), 256)
        wpart[rows, :] = dot(xmat[rows, :], amat[...].reshape(2048, 128))

    loop(0, 4, w_part)
    for c in range(CH):
        wsend[c // 2, pl.ds((c % 2) * 32, 32), :] = wpart[pl.ds(c, 32, stride=32), :].astype(bf16)
    planes(lambda mm: rcopy(wsend.at[mm], wrecv.at[m], w1s.at[mm], w1r.at[m], plane_dev(mm)).start())
    wrecv[m] = wsend[m]

    def back_wait(zz):
        rcopy(rz.at[zrows(zz), :], rzr.at[zz], bzs.at[zz], bzr.at[zz], z_dev(zz)).wait_recv()
        rcopy(lgs.at[zrows(zz), :], lzr.at[zz], bls.at[zz], blr.at[zz], z_dev(zz)).wait_recv()

    zs(back_wait)
    for d in range(16):
        t = rzr[0, :, pl.ds(d * 128, 128)].astype(f32)
        for zz in range(1, NZ):
            t = t + rzr[zz, :, pl.ds(d * 128, 128)].astype(f32)
        bsf[pl.ds(32 + d, 16, stride=48), :] = t
    for zz in range(NZ):
        for xx in range(NX):
            bsf[pl.ds(zz * 4 + xx, 16, stride=48), :] = lzr[zz, :, pl.ds(xx * 128, 128)].astype(f32)
    loop(0, NM, lambda k: bs.__setitem__(k, bsf[pl.ds(pl.multiple_of(k * 48, 48), 48), :].astype(bf16)))
    planes(lambda mm: rcopy(bs.at[mm], br.at[m], b1s.at[mm], b1r.at[m], plane_dev(mm)).start())
    br[m] = bs[m]

    planes(lambda mm: rcopy(wsend.at[mm], wrecv.at[mm], w1s.at[mm], w1r.at[mm], plane_dev(mm)).wait_recv())
    t = wrecv[0].astype(f32)
    for mm in range(1, NM):
        t = t + wrecv[mm].astype(f32)
    wzs[...] = t.reshape(NZ, 8, 128)
    zs(lambda zz: rcopy(wzs.at[zz], wzr.at[z], wzss.at[zz], wzrs.at[z], z_dev(zz)).start())
    wzr[z] = wzs[z]

    planes(lambda mm: rcopy(bs.at[mm], br.at[mm], b1s.at[mm], b1r.at[mm], plane_dev(mm)).wait_recv())
    lparts = []
    for yc in range(4):
        t = None
        for xx in range(NX):
            v = br[(yc // 2) * 8 + xx * 2 + yc % 2, pl.ds(0, 32), :].astype(f32)
            t = v if t is None else t + v
        lparts.append(t)
    lg = jnp.concatenate(lparts, axis=0)
    rparts = []
    for cc in range(2):
        row = []
        for xx in range(NX):
            row.append(br[xx * 2 + cc, pl.ds(32, 16), :].astype(f32) + br[8 + xx * 2 + cc, pl.ds(32, 16), :].astype(f32))
        rparts.append(jnp.concatenate(row, axis=1))
    rg = jnp.concatenate(rparts, axis=0)
    lgb = lg.astype(bf16)
    lgt = lgb.astype(f32).T
    lcat = jnp.concatenate([lgt[r * 32 : r * 32 + 32, :] for r in range(4)], axis=1).astype(bf16)
    rgb = rg.astype(bf16)
    pleft = dot(lcat, np_[...])
    pright = dot(rgb, nb[...])
    for h in range(2):
        cols = slice(h * 128, h * 128 + 128)
        for k in range(4):
            psend[h * 8 + k] = pleft[k * 8 : k * 8 + 8, cols]
            psend[h * 8 + 4 + k] = pright[k * 8 : k * 8 + 8, cols]
    planes(lambda mm: rcopy(psend.at[mm], precv.at[m], p1s.at[mm], p1r.at[m], plane_dev(mm)).start())
    precv[m] = psend[m]

    zs(lambda zz: rcopy(wzs.at[zz], wzr.at[zz], wzss.at[zz], wzrs.at[zz], z_dev(zz)).wait_recv())
    t = wzr[0]
    for zz in range(1, NZ):
        t = t + wzr[zz]
    wzg[z] = t * (math.sqrt(ROWS) / RES)
    zs(lambda zz: rcopy(wzg.at[z], wzg.at[z], wgs.at[zz], wgr.at[z], z_dev(zz)).start())

    row_r = lax.broadcasted_iota(jnp.int32, (128, 256), 0) >> 5
    for r in range(4):
        v = dot(lgb, jnp.where(row_r == r, wl4t[...].astype(f32), 0.0).astype(bf16))
        for yc in range(4):
            start = (yc // 2) * 256 + (yc % 2) * 4 + r
            for h in range(2):
                ng[h, pl.ds(start, 32, stride=8), :] = v[yc * 32 : yc * 32 + 32, h * 128 : h * 128 + 128]
    nr = dot(rgb.astype(f32).T.astype(bf16), wrt[...])
    ng[0] = ng[0] + nr[:, :128]
    ng[1] = ng[1] + nr[:, 128:]

    planes(lambda mm: rcopy(psend.at[mm], precv.at[mm], p1s.at[mm], p1r.at[mm], plane_dev(mm)).wait_recv())
    t = precv[0]
    for mm in range(1, NM):
        t = t + precv[mm]
    pzs[...] = t
    zs(lambda zz: rcopy(pzs, pzr.at[z], pzss.at[zz], pzrs.at[z], z_dev(zz)).start())
    pzr[z] = t

    zs(lambda zz: rcopy(wzg.at[zz], wzg.at[zz], wgs.at[zz], wgr.at[zz], z_dev(zz)).wait_recv())
    mrows = pl.ds(pl.multiple_of(m * 64, 64), 64)
    wfin[...] = wzg[...].reshape(64, 128)
    wo_out[mrows, :] = wfin[...]
    planes(lambda mm: rcopy(wfin, wo_out.at[mrows, :], was.at[mm], war.at[m], plane_dev(mm)).start())

    def back_rows(k):
        rows = pl.ds(pl.multiple_of(k * 64, 64), 64)
        hid = jnp.concatenate([ng[0, rows, :], ng[1, rows, :]], axis=1) * stretch[...]
        sc = scaled[rows, :]
        iv = inv[rows, :][:, :1]
        g = iv * (
            hid - jnp.mean(hid, axis=-1, keepdims=True) - sc * jnp.mean(hid * sc, axis=-1, keepdims=True)
        )
        ag_out[0, rows, :] = g.astype(bf16)

    loop(0, 8, back_rows)

    zs(lambda zz: rcopy(pzs, pzr.at[zz], pzss.at[zz], pzrs.at[zz], z_dev(zz)).wait_recv())
    t = pzr[0]
    for zz in range(1, NZ):
        t = t + pzr[zz]
    t = t * (1.0 / RES)
    pgs[...] = t
    planes(lambda mm: rcopy(pgs, pgr.at[m], pas.at[mm], par.at[m], plane_dev(mm)).start())
    pgr[m] = t
    planes(lambda mm: rcopy(pgs, pgr.at[mm], pas.at[mm], par.at[mm], plane_dev(mm)).wait_recv())
    pt = pgr[...].reshape(128, 128).T
    pg_out[pl.ds(0, 128), :] = pt[:, :64]
    pg_out[pl.ds(128, 128), :] = pt[:, 64:]

    xs(lambda xx: rcopy(pdb.at[pl.ds(xx * 4, 4)], out_part(xx), pds.at[xx], pdr.at[xx], x_dev(xx)).wait_recv())

    def rows_of(mm):
        return wo_out.at[pl.ds(pl.multiple_of(mm * 64, 64), 64), :]

    planes(lambda mm: rcopy(wfin, rows_of(mm), was.at[mm], war.at[mm], plane_dev(mm)).wait_recv())

    def sent_plane(mm):
        dev = plane_dev(mm)
        rcopy(sb.at[mm], rb.at[m], s1s.at[mm], s1r.at[m], dev).wait_send()
        rcopy(wsend.at[mm], wrecv.at[m], w1s.at[mm], w1r.at[m], dev).wait_send()
        rcopy(bs.at[mm], br.at[m], b1s.at[mm], b1r.at[m], dev).wait_send()
        rcopy(psend.at[mm], precv.at[m], p1s.at[mm], p1r.at[m], dev).wait_send()
        rcopy(wfin, wo_out.at[mrows, :], was.at[mm], war.at[m], dev).wait_send()
        rcopy(pgs, pgr.at[m], pas.at[mm], par.at[m], dev).wait_send()

    planes(sent_plane)

    def sent_z(zz):
        dev = z_dev(zz)
        rcopy(ls.at[zz], lmat.at[zrows(z), :], zls.at[zz], zlr.at[z], dev).wait_send()
        rcopy(rs, r_piece(z, core), zrs.at[zz], zrr.at[z], dev).wait_send()
        rcopy(rz.at[zrows(zz), :], rzr.at[z], bzs.at[zz], bzr.at[z], dev).wait_send()
        rcopy(lgs.at[zrows(zz), :], lzr.at[z], bls.at[zz], blr.at[z], dev).wait_send()
        rcopy(wzs.at[zz], wzr.at[z], wzss.at[zz], wzrs.at[z], dev).wait_send()
        rcopy(wzg.at[z], wzg.at[z], wgs.at[zz], wgr.at[z], dev).wait_send()
        rcopy(pzs, pzr.at[z], pzss.at[zz], pzrs.at[z], dev).wait_send()

    zs(sent_z)

    def sent_x(xx):
        dev = x_dev(xx)
        rcopy(adj_part(xx), own_i(x), cps.at[xx], cpr.at[x], dev).wait_send()
        rcopy(pdb.at[pl.ds(xx * 4, 4)], out_part(x), pds.at[xx], pdr.at[x], dev).wait_send()

    xs(sent_x)
    loop(0, NZ, lambda zz: rcopy(r_piece(zz, core), r_piece(zz, core), crs.at[zz], crr.at[zz], core_dev).wait_send())
    rg_copy.wait_send()


def shards(msa, stretch, shift, wlr, offs, wf, fbias, adj):
    def vm(shape, dtype):
        return pltpu.VMEM(shape, dtype)

    def sem(*n):
        return pltpu.SemaphoreType.DMA(n)

    scratch = [
        vm((512, 256), f32), vm((512, 128), f32), vm((2, 512, 128), f32), vm((512, 256), bf16), vm((512, 256), bf16),
        vm((128, 256), bf16), vm((32, 256), bf16), vm((128, 128), bf16), vm((32, 512), bf16),
        vm((16, 48, 128), bf16), vm((16, 48, 128), bf16), vm((768, 128), f32), vm((8, 16, 512), bf16),
        vm((16, 2048), bf16), vm((128, 512), bf16), vm((512, 128), bf16), vm((128, 4096), bf16),
        vm((16, 128, 128), bf16), vm((1024, 128), f32), vm((1024, 128), bf16), vm((128, 1024), bf16),
        vm((512, 4096), bf16), vm((1024, 2048), bf16), vm((128, 2048), bf16), vm((128, 2048), bf16),
        vm((128, 2048), f32), vm((128, 2048), bf16), vm((8, 16, 2048), bf16), vm((128, 512), f32),
        vm((128, 512), bf16), vm((8, 16, 512), bf16), vm((768, 128), f32), vm((16, 48, 128), bf16),
        vm((16, 48, 128), bf16), vm((2, 512, 128), f32),
        vm((1024, 128), f32), vm((16, 64, 128), bf16), vm((16, 64, 128), bf16), vm((8, 8, 128), f32),
        vm((8, 8, 128), f32), vm((8, 8, 128), f32), vm((64, 128), f32), vm((16, 128, 128), bf16),
        vm((16, 8, 128), f32), vm((16, 8, 128), f32), vm((8, 128), f32), vm((8, 8, 128), f32), vm((8, 128), f32),
        vm((16, 8, 128), f32),
        sem(16), sem(16), sem(4), sem(4), sem(8), sem(8), sem(8), sem(8), sem(8), sem(8),
        pltpu.SemaphoreType.DMA, pltpu.SemaphoreType.DMA,
        sem(8), sem(8), sem(8), sem(8), sem(16), sem(16),
        sem(4), sem(4), sem(16), sem(16), sem(8), sem(8), sem(8), sem(8), sem(16), sem(16), sem(16), sem(16),
        sem(8), sem(8), sem(16), sem(16),
    ]
    return pl.pallas_call(
        kernel,
        out_shape=(
            jax.ShapeDtypeStruct((4, 512, 128), bf16),
            jax.ShapeDtypeStruct((1, 512, 256), bf16),
            jax.ShapeDtypeStruct((256, 64), f32),
            jax.ShapeDtypeStruct((1024, 128), f32),
        ),
        in_specs=[pl.BlockSpec(memory_space=pltpu.VMEM)] * 8,
        out_specs=(pl.BlockSpec(memory_space=pltpu.VMEM),) * 4,
        scratch_shapes=scratch,
        compiler_params=pltpu.CompilerParams(
            collective_id=0, has_side_effects=True, vmem_limit_bytes=48 * 1024 * 1024
        ),
    )(
        msa,
        stretch.reshape(1, 256),
        shift.reshape(1, 256),
        wlr,
        offs.reshape(1, 64),
        wf,
        fbias.reshape(1, 128),
        adj,
    )


def solution(mesh):
    placed = (P("dap", "crop", None), P(), P(), P(), P(), P(), P(), P("dap", "crop", None))
    return jax.shard_map(
        shards,
        mesh=mesh,
        in_specs=placed,
        out_specs=(
            P("dap", "crop", None),
            P("dap", "crop", None),
            P("crop", None),
            P("crop", None),
        ),
        check_vma=False,
    )
```

time: 1960 us -> 84.2 us (0.04)
  waiting for transfers between devices: 1760 us -> 0 us
  local copies, waits for them, and re-layouts: 93.1 us -> 6.85 us
  Pallas kernels: 0 us -> 76.4 us
  blocking collectives: 56.1 us -> 0 us
  matrix products: 28.3 us -> 0 us
    psum x1 -> x0, waiting for transfers between devices: 977 us -> none  [shards(): lax.psum((weight_portion, weight_sum), 'dap')]
    reduce_scatter x1 -> x0, waiting for transfers between devices: 569 us -> none  [shards(): lax.psum_scatter(column_buf, 'dap', scatter_dimension=1, tiled=True)]
    all_gather x1 -> x0, waiting for transfers between devices: 209 us -> none  [shards(): piece = lax.all_gather(right_rows, 'dap', axis=1, tiled=True)]
    pallas_call x0 -> x1, Pallas kernels: none -> 76.4 us  [shards(): pl.pallas_call(kernel, out_shape=(jax.ShapeDtypeStruct((4, 512, 128), bf1...]
    all_to_all x2 -> x0, blocking collectives: 56.1 us -> none  [the longest x1 29.7 us: shards(): lax.all_to_all(multiple_sequence_matrix.reshape(homolog_slice, segment_co...]
    reshape x14 -> x0, local copies, waits for them, and re-layouts: 45.5 us -> none  [the longest x4 23.5 us: pair_terms(): regrouped = regrouped.reshape(own_count * chan, feature_depth * chan)]
    dot_general x27 -> x0, matrix products: 28.3 us -> none  [the longest x4 7.21 us: inner(): jnp.dot(left_rows, regrouped, preferred_element_type=jnp.float32)]
    transpose x8 -> x0, local copies, waits for them, and re-layouts: 27.4 us -> none  [the longest x4 14.6 us: pair_terms(): jnp.transpose(outer, (0, 2, 1, 3))]
  transfers between devices with their start and end apart: 3 -> 0, of which waited for: 3 -> 0; matrix products, arithmetic and copies ran while one was open for 0% -> 0% of each run, Pallas kernels for 0% -> 0%
where the time goes in v1:
time: 84.2 us; the launch traced here: 83.9 us
  Pallas kernels  76.4 us (91%)
  local copies, waits for them, and re-layouts  6.85 us (8%)
    pallas_call x1, Pallas kernels, shards(): pl.pallas_call(kernel, out_shape=(jax.ShapeDtypeStruct((4, 512, 128), bf1...  76.4 us
    unnamed x18, local copies, waits for them, and re-layouts  6.13 us

profile of v1, /device:TPU:1, one launch (start us, length us, event | category | flops | bytes accessed | tf_op | source)
XLA Modules:
  0.0 83.9 jit_solution(8173054583508124303)
XLA Ops:
  0.6 0.0 copy-start.3
  0.6 0.0 copy-start.4
  0.7 0.0 copy-start.5
  0.7 0.0 copy-start.6
  0.7 0.9 %copy.12.wlr = bf16[256,64]{1,0:T(8,128)(2,1)S(1)} copy(bf16[256,64]{0,1:T(8,128)(2,1)} %param.11) | data formatting | bytes 65536 | tf_op args[3]
  1.6 0.0 copy-done.3
  1.6 0.0 copy-done.4
  1.6 0.0 copy-done.5
  1.6 0.0 copy-done.6
  1.6 0.0 copy-start
  1.6 1.0 %copy-done = bf16[4,512,128]{2,1,0:T(8,128)(2,1)S(1)} copy-done((bf16[4,512,128]{2,1,0:T(8,128)(2,1)S(1)}, bf16[4,512,128]{2,1,0:T(8,128)(2,1)}, u32[]{:S(2)}) %copy-start) | copy-done | bytes 524312
  2.7 0.0 copy-start.1
  2.7 0.9 %copy-done.1 = bf16[1,512,256]{2,1,0:T(8,128)(2,1)S(1)} copy-done((bf16[1,512,256]{2,1,0:T(8,128)(2,1)S(1)}, bf16[1,512,256]{2,1,0:T(8,128)(2,1)}, u32[]{:S(2)}) %copy-start.1) | copy-done | bytes 262168
  3.6 0.0 copy-start.2
  3.6 0.9 %copy-done.2 = bf16[1024,128]{1,0:T(8,128)(2,1)S(1)} copy-done((bf16[1024,128]{1,0:T(8,128)(2,1)S(1)}, bf16[1024,128]{1,0:T(8,128)(2,1)}, u32[]{:S(2)}) %copy-start.2) | copy-done | bytes 262168
  4.6 76.4 %shard_map.111 = (bf16[4,512,128]{2,1,0:T(8,128)(2,1)S(1)}, bf16[1,512,256]{2,1,0:T(8,128)(2,1)S(1)}, f32[256,64]{1,0:T(8,128)S(1)}, f32[1024,128]{1,0:T(8,128)S(1)}) custom-call(bf16[1,512,256]{2,1,0:T(8,128)(2,1)S(1)} %copy-done.1, f32[1,256]{1,0:T(1,128)S(1)} %bitcast.4, f32[1,256]{1,0:T(1,128)S(1)} %bitcast.5, bf16[256,64]{1,0:T(8,128)(2,1)S(1)} %copy.12.wlr, ...), custom_call_target="tpu_custom_call" | custom-call | tf_op jit(solution)/shard_map/pallas_call | solution.py:443
  80.9 0.7 copy.13
  81.7 0.8 copy.17
  82.4 0.7 copy.18
  83.2 0.8 copy.19
Async XLA Ops:
  0.6 0.9 %copy-start.3 = (f32[256]{0:T(256)S(1)}, f32[256]{0:T(256)}, u32[]{:S(2)}) copy-start(f32[256]{0:T(256)} %param.9) | copy-start | bytes 3076
  0.6 0.9 %copy-start.4 = (f32[256]{0:T(256)S(1)}, f32[256]{0:T(256)}, u32[]{:S(2)}) copy-start(f32[256]{0:T(256)} %param.10) | copy-start | bytes 3076
  0.7 0.9 %copy-start.5 = (f32[64]{0:T(128)S(1)}, f32[64]{0:T(128)}, u32[]{:S(2)}) copy-start(f32[64]{0:T(128)} %param.12) | copy-start | bytes 772
  0.7 0.9 %copy-start.6 = (f32[128]{0:T(128)S(1)}, f32[128]{0:T(128)}, u32[]{:S(2)}) copy-start(f32[128]{0:T(128)} %param.14) | copy-start | bytes 1540
  1.6 1.0 %copy-start = (bf16[4,512,128]{2,1,0:T(8,128)(2,1)S(1)}, bf16[4,512,128]{2,1,0:T(8,128)(2,1)}, u32[]{:S(2)}) copy-start(bf16[4,512,128]{2,1,0:T(8,128)(2,1)} %adj.1) | copy-start | bytes 1572868
  2.7 0.9 %copy-start.1 = (bf16[1,512,256]{2,1,0:T(8,128)(2,1)S(1)}, bf16[1,512,256]{2,1,0:T(8,128)(2,1)}, u32[]{:S(2)}) copy-start(bf16[1,512,256]{2,1,0:T(8,128)(2,1)} %msa.1) | copy-start | bytes 786436
  3.6 0.9 %copy-start.2 = (bf16[1024,128]{1,0:T(8,128)(2,1)S(1)}, bf16[1024,128]{1,0:T(8,128)(2,1)}, u32[]{:S(2)}) copy-start(bf16[1024,128]{1,0:T(8,128)(2,1)} %wf.1) | copy-start | bytes 786436

commit v2 on v1

v2 whole, which is shorter than its diff:
```python
import math

import jax
import jax.numpy as jnp
from jax import lax
from jax.experimental import pallas as pl
from jax.experimental.pallas import tpu as pltpu
from jax.sharding import PartitionSpec as P

EPSILON = 1e-05
MESH = pl.DeviceIdType.MESH
f32 = jnp.float32
bf16 = jnp.bfloat16

NX, NZ, NM = 4, 8, 16
CH = 32
ROWS = 128
RES = 512


def dot(a, b):
    return jnp.dot(a, b, preferred_element_type=f32)


def dot_nt(a, b):
    return lax.dot_general(a, b, (((1,), (1,)), ((), ())), preferred_element_type=f32)


def loop(low, high, body):
    def step(k, carry):
        body(k)
        return carry

    lax.fori_loop(low, high, step, 0)


class Exchange:
    def __init__(self, each, device, mine, src, dst, whole, ssem, rsem, apart=False):
        self.each, self.device, self.mine, self.src, self.dst, self.whole = each, device, mine, src, dst, whole
        self.ssem, self.rsem, self.apart = ssem, rsem, apart
        self.waited = False

    def copy(self, p, slot):
        return pltpu.make_async_remote_copy(
            src_ref=self.src(p),
            dst_ref=self.dst(slot),
            send_sem=self.ssem.at[0],
            recv_sem=self.rsem.at[slot if self.apart else 0],
            device_id={"dap": self.device(p)},
            device_id_type=MESH,
        )

    def bulk(self):
        return pltpu.make_async_remote_copy(
            src_ref=self.whole,
            dst_ref=self.whole,
            send_sem=self.ssem.at[0],
            recv_sem=self.rsem.at[0],
            device_id={"dap": self.device(0)},
            device_id_type=MESH,
        )

    def start_one(self, p):
        self.copy(p, self.mine).start()

    def recv_one(self, p):
        self.copy(p, p).wait_recv()

    def start(self):
        self.each(self.start_one)

    def recv(self):
        self.waited = True
        if self.apart:
            self.each(self.recv_one)
        else:
            self.bulk().wait_recv()

    def sent(self):
        self.bulk().wait_send()


def kernel(
    msa_h, stretch_h, shift_h, wlrt_h, offs_h, wf_h, fbias_h, adj_h,
    pd_h, ag_h, pg_h, wo_h,
    pd_out, ag_out, pg_out, wo_out,
    msa, stretch, shift, wlrt_v, offs, wf, fbias, adj,
    scaled, inv, nf, nb, np_, wl4t, wrt, lrow, rt,
    sb, rb, rbf, ls, rs, lmat, lt, rmat, amat, wff, w2, w2t,
    gmat, xmat, rgs, rgr, rgo, ryq, ryr, rz, rzr, lacc, lgs, lzr, bsf, bs, br, ng,
    wpart, wsend, wrecv, wzs, wzr, wfin, wall_v, pdb,
    psend, precv, pzs, pzr, pgs, pgr,
    in_sem, adj_sem, ssems, rsems, adj_r, zr_r, yf_r, ry_r,
):
    me = lax.axis_index("dap")
    core = lax.rem(me, 2)
    x = lax.rem(me // 2, NX)
    z = lax.rem(me // 8, NZ)
    y = me // 64
    m = y * 8 + x * 2 + core
    other = 1 - core

    def plane_dev(mm):
        return (mm // 8) * 64 + z * 8 + lax.rem(mm, 8)

    def z_dev(zz):
        return y * 64 + zz * 8 + x * 2 + core

    def x_dev(xx):
        return y * 64 + z * 8 + xx * 2 + core

    def core_dev(_):
        return y * 64 + z * 8 + x * 2 + other

    def y_dev(_):
        return (1 - y) * 64 + z * 8 + x * 2 + core

    def planes(body):
        loop(1, NM, lambda k: body(lax.rem(m + k, NM)))

    def zs(body):
        for k in (4, 3, 5, 2, 6, 1, 7):
            body(lax.rem(z + k, NZ))

    def xs(body):
        for k in (1, 3, 2):
            body(lax.rem(x + k, NX))

    exchanges = []

    def exchange(each, device, mine, src, dst, whole, rsem=None):
        k = pl.ds(len(exchanges), 1)
        e = Exchange(
            each, device, mine, src, dst, whole, ssems.at[k], rsems.at[k] if rsem is None else rsem, rsem is not None
        )
        exchanges.append(e)
        return e

    def finish():
        for e in exchanges:
            if not e.waited:
                e.recv()
        for e in exchanges:
            e.sent()

    small = [
        pltpu.make_async_copy(src, dst, in_sem.at[k])
        for k, (src, dst) in enumerate(
            [
                (msa_h, msa), (stretch_h, stretch), (shift_h, shift), (wlrt_h, wlrt_v), (offs_h, offs),
                (wf_h, wf), (fbias_h, fbias), (adj_h, adj),
            ]
        )
    ]
    for c in small:
        c.start()

    def adj_part(xx):
        return adj.at[:, pl.ds(pl.multiple_of(xx * 128, 128), 128), :]

    def own_i(xx):
        return amat.at[pl.ds(xx * 4, 4)]


    barrier = pltpu.get_barrier_semaphore()
    planes(lambda mm: pl.semaphore_signal(barrier, inc=1, device_id={"dap": plane_dev(mm)}, device_id_type=MESH))
    zs(lambda zz: pl.semaphore_signal(barrier, inc=1, device_id={"dap": z_dev(zz)}, device_id_type=MESH))
    for c in small:
        c.wait()

    def norm_rows(k):
        rows = pl.ds(pl.multiple_of(k * 64, 64), 64)
        v = msa[0, rows, :].astype(f32)
        c = v - jnp.mean(v, axis=-1, keepdims=True)
        iv = lax.rsqrt(jnp.mean(c * c, axis=-1, keepdims=True) + EPSILON)
        sc = c * iv
        scaled[rows, :] = sc
        inv[rows, :] = jnp.broadcast_to(iv, (64, 128))
        n = (sc * stretch[...] + shift[...]).astype(bf16)
        nb[rows, :] = n
        n = n.astype(f32)
        nf[0, rows, :] = n[:, :128]
        nf[1, rows, :] = n[:, 128:]

    loop(0, 8, norm_rows)
    for r in range(4):
        for yc in range(4):
            start = (yc // 2) * 256 + (yc % 2) * 4 + r
            for h in range(2):
                np_[pl.ds(r * 128 + yc * 32, 32), pl.ds(h * 128, 128)] = nf[
                    h, pl.ds(start, 32, stride=8), :
                ].astype(bf16)

    wlrt = wlrt_v[...]
    w_rows = wlrt.astype(f32).T.astype(bf16)
    wrt[...] = wlrt[CH:, :]
    spread = lax.broadcasted_iota(jnp.int32, (64, 128), 0) == (lax.broadcasted_iota(jnp.int32, (64, 128), 1) & 31)
    wl4 = dot(w_rows, spread.astype(f32).astype(bf16))
    wl4t[...] = wl4.T.astype(bf16)
    diag = lax.broadcasted_iota(jnp.int32, (64, 64), 0) == lax.broadcasted_iota(jnp.int32, (64, 64), 1)
    offs_col = jnp.sum(jnp.where(diag, jnp.broadcast_to(offs[...], (64, 64)), 0.0), axis=1, keepdims=True)
    offs4 = jnp.sum(jnp.where(spread, jnp.broadcast_to(offs_col, (64, 128)), 0.0), axis=0, keepdims=True)
    lane_r = lax.broadcasted_iota(jnp.int32, (256, 128), 1) >> 5
    left = jnp.zeros((128, 128), f32)
    for r in range(4):
        left = left + dot(np_[pl.ds(r * 128, 128), :], jnp.where(lane_r == r, wl4, 0.0).astype(bf16))
    lrow[...] = (left + offs4).astype(bf16)
    rt[...] = (dot_nt(wlrt[CH:, :], nb[...]) + offs_col[CH:, :]).astype(bf16)
    for mm in range(NM):
        yc = (mm // 8) * 2 + mm % 2
        xx, cc = (mm % 8) // 2, mm % 2
        sb[mm, pl.ds(0, 32), :] = lrow[pl.ds(yc * 32, 32), :]
        sb[mm, pl.ds(32, 16), :] = rt[pl.ds(cc * 16, 16), pl.ds(xx * 128, 128)]

    pl.semaphore_wait(barrier, NM - 1 + NZ - 1)

    first = exchange(planes, plane_dev, m, lambda mm: sb.at[mm], lambda mm: rb.at[mm], rb.at[pl.ds(0, NM - 1)])
    first.start()
    rb[m] = sb[m]
    adjoint = exchange(xs, x_dev, x, adj_part, own_i, amat.at[pl.ds(0, 12)], adj_r)
    adjoint.start()
    own_adj = pltpu.make_async_copy(adj_part(x), own_i(x), adj_sem)
    own_adj.start()

    wff[...] = wf[...].astype(f32)
    for d in range(CH):
        w2[pl.ds(d * 32, 32), :] = wff[pl.ds(d, 32, stride=32), :].astype(bf16)
    for k in range(8):
        w2t[:, pl.ds(k * 128, 128)] = w2[pl.ds(k * 128, 128), :].astype(f32).T.astype(bf16)

    first.recv()

    loop(0, NM, lambda k: rbf.__setitem__((pl.ds(pl.multiple_of(k * 48, 48), 48), slice(None)), rb[k].astype(f32)))
    for zz in range(NZ):
        for xx in range(NX):
            ls[zz, :, pl.ds(xx * 128, 128)] = (rbf[pl.ds(zz * 4 + xx, 16, stride=48), :] * (1.0 / ROWS)).astype(bf16)
    for d in range(16):
        rs[:, pl.ds(d * 128, 128)] = rbf[pl.ds(32 + d, 16, stride=48), :].astype(bf16)

    def zrows(zz):
        return pl.ds(pl.multiple_of(zz * 16, 16), 16)

    def half(cc):
        return pl.ds(pl.multiple_of(cc * 2048, 2048), 2048)

    def quarter(cc, yy):
        return pl.ds(pl.multiple_of(cc * 2048 + yy * 1024, 1024), 1024)

    def r_piece(zz, yy):
        return rmat.at[zrows(zz), quarter(core, yy)]

    zleft = exchange(
        zs, z_dev, z, lambda zz: ls.at[zz], lambda zz: lmat.at[zrows(zz), :], lmat.at[pl.ds(0, 112), :]
    )
    zleft.start()
    rs_own = rs.at[:, pl.ds(pl.multiple_of(y * 1024, 1024), 1024)]
    zright = exchange(
        zs, z_dev, z, lambda zz: rs_own, lambda zz: r_piece(zz, y), rmat.at[pl.ds(0, 112), quarter(core, y)], zr_r
    )
    zright.start()
    lmat[zrows(z), :] = ls[z]
    rmat[zrows(z), half(core)] = rs[...]

    yswap = exchange(
        zs, y_dev, None, lambda zz: r_piece(zz, y), None, rmat.at[pl.ds(0, 112), quarter(core, y)], yf_r
    )
    swap = exchange(None, core_dev, None, None, None, rmat.at[:, half(other)])

    def to_core(piece):
        pltpu.make_async_remote_copy(
            src_ref=piece,
            dst_ref=piece,
            send_sem=swap.ssem.at[0],
            recv_sem=swap.rsem.at[0],
            device_id={"dap": core_dev(0)},
            device_id_type=MESH,
        ).start()

    def y_copy(zz, yy):
        return pltpu.make_async_remote_copy(
            src_ref=r_piece(zz, yy),
            dst_ref=r_piece(zz, yy),
            send_sem=yswap.ssem.at[0],
            recv_sem=yf_r.at[zz],
            device_id={"dap": y_dev(0)},
            device_id_type=MESH,
        )

    yswap.recv_one = lambda zz: y_copy(zz, 1 - y).wait_recv()

    def forward(k):
        zz = lax.rem(z + k, NZ)
        zright.recv_one(zz)
        y_copy(zz, y).start()
        to_core(r_piece(zz, y))

    def forward_y(k):
        zz = lax.rem(z + k, NZ)
        yswap.recv_one(zz)
        to_core(r_piece(zz, 1 - y))

    to_core(rmat.at[zrows(z), half(core)])
    zright.waited = True
    yswap.waited = True

    def grad_pair(t):
        a2 = amat[pl.ds(t * 2, 2)].reshape(256, 128)
        for q in range(4):
            g = dot_nt(w2[pl.ds(q * 256, 256), :], a2)
            for e in range(8):
                for u in range(2):
                    rows = pl.ds(pl.multiple_of((2 * t + u) * 32, 32), 32)
                    gmat[rows, pl.ds((q * 8 + e) * 128, 128)] = g[e * 32 : e * 32 + 32, u * 128 : u * 128 + 128].astype(
                        bf16
                    )

    own_adj.wait()
    loop(x * 2, x * 2 + 2, grad_pair)
    adjoint.waited = True
    for k in (1, 3, 2):
        xx = lax.rem(x + k, NX)
        adjoint.recv_one(xx)
        loop(xx * 2, xx * 2 + 2, grad_pair)

    zleft.recv()
    for k in range(4):
        lt[pl.ds(k * 128, 128), :] = lmat[:, pl.ds(k * 128, 128)].astype(f32).T.astype(bf16)

    def right_other(yy):
        def part(k):
            cols = pl.ds(pl.multiple_of(other * 2048 + yy * 1024 + k * 512, 512), 512)
            rgs[:, pl.ds(pl.multiple_of(yy * 1024 + k * 512, 512), 512)] = dot(lmat[...], gmat[:, cols]).astype(bf16)

        loop(0, 2, part)

    def columns(ref, yy):
        return ref.at[:, pl.ds(pl.multiple_of(yy * 1024, 1024), 1024)]

    add = [
        exchange(lambda body: body(0), core_dev, 0, lambda _: columns(rgs, 1 - y), lambda _: columns(rgr, 1 - y), columns(rgr, 1 - y)),
        exchange(lambda body: body(0), core_dev, 0, lambda _: columns(rgs, y), lambda _: columns(rgr, y), columns(rgr, y)),
    ]
    right_other(1 - y)
    add[0].start()
    right_other(y)
    add[1].start()

    def right_own(k):
        cols = pl.ds(pl.multiple_of(core * 2048 + k * 512, 512), 512)
        rgo[:, pl.ds(pl.multiple_of(k * 512, 512), 512)] = dot(lmat[...], gmat[:, cols])

    loop(0, 4, right_own)
    for k in (4, 3, 5, 2):
        forward(k)
    add[0].recv()

    def right_add(k):
        cols = pl.ds(pl.multiple_of((1 - y) * 1024 + k * 512, 512), 512)
        ryq[:, pl.ds(pl.multiple_of(k * 512, 512), 512)] = (rgo[:, cols] + rgr[:, cols].astype(f32)).astype(bf16)

    loop(0, 2, right_add)

    def all_z(body):
        for k in (4, 3, 5, 2, 6, 1, 7, 0):
            body(lax.rem(z + k, NZ))

    ry = exchange(all_z, y_dev, None, lambda zz: ryq.at[zrows(zz), :], None, ryr, ry_r)
    ry.copy = lambda zz, _: pltpu.make_async_remote_copy(
        src_ref=ryq.at[zrows(zz), :],
        dst_ref=ryr.at[zrows(zz), :],
        send_sem=ry.ssem.at[0],
        recv_sem=ry_r.at[zz],
        device_id={"dap": y_dev(0)},
        device_id_type=MESH,
    )
    ry.start()
    for k in (6, 1, 7):
        forward(k)
    add[1].recv()

    for k in (4, 3, 5, 2, 6, 1, 7):
        forward_y(k)
    swap.recv()

    bright = exchange(
        zs, z_dev, z, lambda zz: rz.at[zrows(zz), :], lambda zz: rzr.at[zz], rzr.at[pl.ds(0, NZ - 1)]
    )
    mine = pl.ds(pl.multiple_of(y * 1024, 1024), 1024)
    ry.waited = True

    def right_rows(k):
        zz = lax.rem(z + k, NZ)
        ry.recv_one(zz)
        t = rgo[zrows(zz), mine] + rgr[zrows(zz), mine].astype(f32) + ryr[zrows(zz), :].astype(f32)
        if k == 0:
            rzr[z] = t.astype(bf16)
        else:
            rz[zrows(zz), :] = t.astype(bf16)
            bright.start_one(zz)

    lacc[...] = jnp.zeros((128, 512), f32)
    for n, ks in enumerate([(4, 3), (5, 2), (6, 1), (7, 0)]):
        lacc[...] += dot_nt(rmat[:, pl.ds(n * 1024, 1024)], gmat[:, pl.ds(n * 1024, 1024)])
        for k in ks:
            right_rows(k)
    lgs[...] = (lacc[...] * (1.0 / ROWS)).astype(bf16)
    bleft = exchange(
        zs, z_dev, z, lambda zz: lgs.at[zrows(zz), :], lambda zz: lzr.at[zz], lzr.at[pl.ds(0, NZ - 1)]
    )
    bleft.start()
    lzr[z] = lgs[zrows(z), :]

    def outer_part(n):
        o = dot(lt[...], rmat[:, pl.ds(pl.multiple_of(n * 256, 256), 256)])
        for i in range(16):
            for e in range(2):
                rows = pl.ds(pl.multiple_of((2 * n + e) * 32, 32), 32)
                xmat[rows, pl.ds(i * 128, 128)] = o[i * 32 : i * 32 + 32, e * 128 : e * 128 + 128].astype(bf16)

    loop(0, 16, outer_part)

    def delta_pair(t):
        p = dot(w2t[...], xmat[:, pl.ds(pl.multiple_of(t * 256, 256), 256)])
        pdb[pl.ds(t * 2, 2)] = (p.T + fbias[...]).astype(bf16).reshape(2, 128, 128)

    loop(0, 8, delta_pair)

    def out_part(xx):
        return pd_out.at[:, pl.ds(pl.multiple_of(xx * 128, 128), 128), :]

    delta = exchange(xs, x_dev, x, lambda xx: pdb.at[pl.ds(xx * 4, 4)], out_part, pd_out.at[:, pl.ds(0, 384), :])
    delta.start()
    pd_out[:, pl.ds(pl.multiple_of(x * 128, 128), 128), :] = pdb[pl.ds(x * 4, 4)]

    def w_part(n):
        rows = pl.ds(pl.multiple_of(n * 256, 256), 256)
        wpart[rows, :] = dot(xmat[rows, :], amat[...].reshape(2048, 128))

    loop(0, 4, w_part)
    for c in range(CH):
        wsend[c // 2, pl.ds((c % 2) * 32, 32), :] = wpart[pl.ds(c, 32, stride=32), :].astype(bf16)
    wplane = exchange(planes, plane_dev, m, lambda mm: wsend.at[mm], lambda mm: wrecv.at[mm], wrecv.at[pl.ds(0, NM - 1)])
    wplane.start()
    wrecv[m] = wsend[m]

    bright.recv()
    bleft.recv()
    bsf[...] = jnp.zeros((768, 128), f32)
    for d in range(8):
        t = rzr[0, :, pl.ds(d * 128, 128)].astype(f32)
        for zz in range(1, NZ):
            t = t + rzr[zz, :, pl.ds(d * 128, 128)].astype(f32)
        bsf[pl.ds(32 + d, 16, stride=48), :] = t
    for zz in range(NZ):
        for xx in range(NX):
            bsf[pl.ds(zz * 4 + xx, 16, stride=48), :] = lzr[zz, :, pl.ds(xx * 128, 128)].astype(f32)
    loop(0, NM, lambda k: bs.__setitem__(k, bsf[pl.ds(pl.multiple_of(k * 48, 48), 48), :].astype(bf16)))
    back = exchange(planes, plane_dev, m, lambda mm: bs.at[mm], lambda mm: br.at[mm], br.at[pl.ds(0, NM - 1)])
    back.start()
    br[m] = bs[m]

    back.recv()
    lparts = []
    for yc in range(4):
        t = None
        for xx in range(NX):
            v = br[(yc // 2) * 8 + xx * 2 + yc % 2, pl.ds(0, 32), :].astype(f32)
            t = v if t is None else t + v
        lparts.append(t)
    lg = jnp.concatenate(lparts, axis=0)
    rparts = []
    for cc in range(2):
        for yy in range(2):
            row = [br[yy * 8 + xx * 2 + cc, pl.ds(32, 16), :].astype(f32)[:8] for xx in range(NX)]
            rparts.append(jnp.concatenate(row, axis=1))
    rg = jnp.concatenate(rparts, axis=0)
    lgb = lg.astype(bf16)
    lgt = lgb.astype(f32).T
    lcat = jnp.concatenate([lgt[r * 32 : r * 32 + 32, :] for r in range(4)], axis=1).astype(bf16)
    rgb = rg.astype(bf16)
    pleft = dot(lcat, np_[...])
    pright = dot(rgb, nb[...])
    for h in range(2):
        cols = slice(h * 128, h * 128 + 128)
        for k in range(4):
            psend[h * 8 + k] = pleft[k * 8 : k * 8 + 8, cols]
            psend[h * 8 + 4 + k] = pright[k * 8 : k * 8 + 8, cols]
    pplane = exchange(planes, plane_dev, m, lambda mm: psend.at[mm], lambda mm: precv.at[mm], precv.at[pl.ds(0, NM - 1)])
    pplane.start()
    precv[m] = psend[m]

    wplane.recv()
    t = wrecv[0].astype(f32)
    for mm in range(1, NM):
        t = t + wrecv[mm].astype(f32)
    wzs[...] = t.astype(bf16)
    wz = exchange(zs, z_dev, z, lambda zz: wzs, lambda zz: wzr.at[zz], wzr.at[pl.ds(0, NZ - 1)])
    wz.start()
    wzr[z] = wzs[...]

    row_r = lax.broadcasted_iota(jnp.int32, (128, 256), 0) >> 5
    for r in range(4):
        v = dot(lgb, jnp.where(row_r == r, wl4t[...].astype(f32), 0.0).astype(bf16))
        for yc in range(4):
            start = (yc // 2) * 256 + (yc % 2) * 4 + r
            for h in range(2):
                ng[h, pl.ds(start, 32, stride=8), :] = v[yc * 32 : yc * 32 + 32, h * 128 : h * 128 + 128]
    nr = dot(rgb.astype(f32).T.astype(bf16), wrt[...])
    ng[0] = ng[0] + nr[:, :128]
    ng[1] = ng[1] + nr[:, 128:]

    pplane.recv()
    t = precv[0]
    for mm in range(1, NM):
        t = t + precv[mm]
    pzs[...] = t
    pz = exchange(zs, z_dev, z, lambda zz: pzs, lambda zz: pzr.at[zz], pzr.at[pl.ds(0, NZ - 1)])
    pz.start()
    pzr[z] = t
    def back_rows(k):
        rows = pl.ds(pl.multiple_of(k * 64, 64), 64)
        hid = jnp.concatenate([ng[0, rows, :], ng[1, rows, :]], axis=1) * stretch[...]
        sc = scaled[rows, :]
        iv = inv[rows, :][:, :1]
        g = iv * (
            hid - jnp.mean(hid, axis=-1, keepdims=True) - sc * jnp.mean(hid * sc, axis=-1, keepdims=True)
        )
        ag_out[0, rows, :] = g.astype(bf16)

    loop(0, 8, back_rows)
    ag_copy = pltpu.make_async_copy(ag_out, ag_h, in_sem.at[0])
    ag_copy.start()

    wz.recv()
    t = wzr[0].astype(f32)
    for zz in range(1, NZ):
        t = t + wzr[zz].astype(f32)
    wfin[...] = (t * (math.sqrt(ROWS) / RES)).astype(bf16)
    wall = exchange(
        planes, plane_dev, m, lambda mm: wfin, lambda mm: wall_v.at[mm], wall_v.at[pl.ds(0, NM - 1)]
    )
    wall.start()
    wall_v[m] = wfin[...]

    pz.recv()
    t = pzr[0]
    for zz in range(1, NZ):
        t = t + pzr[zz]
    t = t * (1.0 / RES)
    pgs[...] = t
    pall = exchange(planes, plane_dev, m, lambda mm: pgs, lambda mm: pgr.at[mm], pgr.at[pl.ds(0, NM - 1)])
    pall.start()
    pgr[m] = t

    delta.recv()
    pd_copy = pltpu.make_async_copy(pd_out, pd_h, in_sem.at[1])
    pd_copy.start()
    wall.recv()
    wo_out[...] = wall_v[...].reshape(1024, 128).astype(f32)
    wo_copy = pltpu.make_async_copy(wo_out, wo_h, in_sem.at[2])
    wo_copy.start()
    pall.recv()
    pt = pgr[...].reshape(2, 64, 128)
    pg_out[:, pl.ds(0, 128)] = pt[0]
    pg_out[:, pl.ds(128, 128)] = pt[1]
    pg_copy = pltpu.make_async_copy(pg_out, pg_h, in_sem.at[3])
    pg_copy.start()
    finish()
    for c in (ag_copy, pd_copy, wo_copy, pg_copy):
        c.wait()


def emit(pd, ag, pg, wo, pd_o, ag_o, pg_o, wo_o, pd_v, ag_v, pg_v, wo_v, sems):
    parts = [(pd.at[k], pd_v.at[k], pd_o.at[k]) for k in range(4)]
    parts += [(ag, ag_v, ag_o), (pg, pg_v, pg_o), (wo, wo_v, wo_o)]
    for k, (src, mid, _) in enumerate(parts):
        pltpu.make_async_copy(src, mid, sems.at[k]).start()
    for k, (src, mid, dst) in enumerate(parts):
        pltpu.make_async_copy(src, mid, sems.at[k]).wait()
        pltpu.make_async_copy(mid, dst, sems.at[k]).start()
    for k, (_, mid, dst) in enumerate(parts):
        pltpu.make_async_copy(mid, dst, sems.at[k]).wait()


def shards(msa, stretch, shift, wlr, offs, wf, fbias, adj):
    def vm(shape, dtype):
        return pltpu.VMEM(shape, dtype)

    def sem(*n):
        return pltpu.SemaphoreType.DMA(n)

    scratch = [
        vm((4, 512, 128), bf16), vm((1, 512, 256), bf16), vm((64, 256), f32), vm((1024, 128), f32),
        vm((1, 512, 256), bf16), vm((1, 256), f32), vm((1, 256), f32), vm((64, 256), bf16), vm((1, 64), f32),
        vm((1024, 128), bf16), vm((1, 128), f32), vm((4, 512, 128), bf16),
        vm((512, 256), f32), vm((512, 128), f32), vm((2, 512, 128), f32), vm((512, 256), bf16), vm((512, 256), bf16),
        vm((128, 256), bf16), vm((32, 256), bf16), vm((128, 128), bf16), vm((32, 512), bf16),
        vm((16, 48, 128), bf16), vm((16, 48, 128), bf16), vm((768, 128), f32), vm((8, 16, 512), bf16),
        vm((16, 2048), bf16), vm((128, 512), bf16), vm((512, 128), bf16), vm((128, 4096), bf16),
        vm((16, 128, 128), bf16), vm((1024, 128), f32), vm((1024, 128), bf16), vm((128, 1024), bf16),
        vm((512, 4096), bf16), vm((1024, 2048), bf16), vm((128, 2048), bf16), vm((128, 2048), bf16),
        vm((128, 2048), f32), vm((128, 1024), bf16), vm((128, 1024), bf16), vm((128, 1024), bf16),
        vm((8, 16, 1024), bf16), vm((128, 512), f32),
        vm((128, 512), bf16), vm((8, 16, 512), bf16), vm((768, 128), f32), vm((16, 48, 128), bf16),
        vm((16, 48, 128), bf16), vm((2, 512, 128), f32),
        vm((1024, 128), f32), vm((16, 64, 128), bf16), vm((16, 64, 128), bf16), vm((64, 128), bf16),
        vm((8, 64, 128), bf16), vm((64, 128), bf16), vm((16, 64, 128), bf16), vm((16, 128, 128), bf16),
        vm((16, 8, 128), f32), vm((16, 8, 128), f32), vm((8, 128), f32), vm((8, 8, 128), f32), vm((8, 128), f32),
        vm((16, 8, 128), f32),
        sem(8), pltpu.SemaphoreType.DMA, sem(20), sem(20), sem(4), sem(8), sem(8), sem(8),
    ]
    pd, ag, pg, wo = pl.pallas_call(
        kernel,
        out_shape=(
            jax.ShapeDtypeStruct((4, 512, 128), bf16),
            jax.ShapeDtypeStruct((1, 512, 256), bf16),
            jax.ShapeDtypeStruct((64, 256), f32),
            jax.ShapeDtypeStruct((1024, 128), f32),
        ),
        in_specs=[pl.BlockSpec(memory_space=pltpu.HBM)] * 8,
        out_specs=(pl.BlockSpec(memory_space=pltpu.HBM),) * 4,
        scratch_shapes=scratch,
        compiler_params=pltpu.CompilerParams(
            collective_id=0, has_side_effects=True, vmem_limit_bytes=60 * 1024 * 1024
        ),
    )(
        msa,
        stretch.reshape(1, 256),
        shift.reshape(1, 256),
        wlr.T,
        offs.reshape(1, 64),
        wf,
        fbias.reshape(1, 128),
        adj,
    )
    pd, ag, pg, wo = pl.pallas_call(
        emit,
        out_shape=tuple(jax.ShapeDtypeStruct(v.shape, v.dtype) for v in (pd, ag, pg, wo)),
        in_specs=[pl.BlockSpec(memory_space=pltpu.HBM)] * 4,
        out_specs=(pl.BlockSpec(memory_space=pltpu.HBM),) * 4,
        scratch_shapes=[vm((4, 512, 128), bf16), vm((1, 512, 256), bf16), vm((64, 256), f32), vm((1024, 128), f32), sem(7)],
        compiler_params=pltpu.CompilerParams(vmem_limit_bytes=60 * 1024 * 1024),
    )(pd, ag, pg, wo)
    return pd, ag, pg.T, wo


def solution(mesh):
    placed = (P("dap", "crop", None), P(), P(), P(), P(), P(), P(), P("dap", "crop", None))
    return jax.shard_map(
        shards,
        mesh=mesh,
        in_specs=placed,
        out_specs=(
            P("dap", "crop", None),
            P("dap", "crop", None),
            P("crop", None),
            P("crop", None),
        ),
        check_vma=False,
    )
```

time: 84.2 us -> 75.4 us (0.90)
  local copies, waits for them, and re-layouts: 6.85 us -> 0 us
  Pallas kernels: 76.4 us -> 74.7 us
    unnamed x18 -> x0, local copies, waits for them, and re-layouts: 6.13 us -> none
    pallas_call x1, Pallas kernels: 76.4 us -> 72.4 us  [shards(): pl.pallas_call(kernel, out_shape=(jax.ShapeDtypeStruct((4, 512, 128), bf1...]
    pallas_call x0 -> x1, Pallas kernels: none -> 2.26 us  [shards(): pl.pallas_call(emit, out_shape=tuple((jax.ShapeDtypeStruct(v.shape, v.dty...]
where the time goes in v2:
time: 75.4 us; the launch traced here: 75.3 us
  Pallas kernels  74.7 us (99%)
    pallas_call x1, Pallas kernels, shards(): pl.pallas_call(kernel, out_shape=(jax.ShapeDtypeStruct((4, 512, 128), bf1...  72.4 us
    pallas_call x1, Pallas kernels, shards(): pl.pallas_call(emit, out_shape=tuple((jax.ShapeDtypeStruct(v.shape, v.dty...  2.26 us

profile of v2, /device:TPU:1, one launch (start us, length us, event | category | flops | bytes accessed | tf_op | source)
XLA Modules:
  0.0 75.3 jit_solution(10503216507671940921)
XLA Ops:
  0.6 72.4 %shard_map.111 = (bf16[4,512,128]{2,1,0:T(8,128)(2,1)}, bf16[1,512,256]{2,1,0:T(8,128)(2,1)}, f32[64,256]{1,0:T(8,128)}, f32[1024,128]{1,0:T(8,128)}) custom-call(bf16[1,512,256]{2,1,0:T(8,128)(2,1)} %msa_h.1, f32[1,256]{1,0:T(1,128)} %bitcast.7, f32[1,256]{1,0:T(1,128)} %bitcast.8, bf16[64,256]{1,0:T(8,128)(2,1)} %bitcast.6, f32[1,64]{1,0:T(1,128)} %bitcast.9, ...), custom_call_target="tpu_custom_call" | custom-call | tf_op jit(solution)/shard_map/pallas_call | solution.py:612
  73.0 2.3 %shard_map.112 = (bf16[4,512,128]{2,1,0:T(8,128)(2,1)}, bf16[1,512,256]{2,1,0:T(8,128)(2,1)}, f32[64,256]{1,0:T(8,128)}, f32[1024,128]{1,0:T(8,128)}) custom-call(bf16[4,512,128]{2,1,0:T(8,128)(2,1)} %get-tuple-element.12.pd, bf16[1,512,256]{2,1,0:T(8,128)(2,1)} %get-tuple-element.13.ag, f32[64,256]{1,0:T(8,128)} %get-tuple-element.14.pg, ...), custom_call_target="tpu_custom_call" | custom-call | tf_op jit(solution)/shard_map/pallas_call | solution.py:636

commit v3 on v2

--- a/solution.py
+++ b/solution.py
@@ -16,6 +16,8 @@
 CH = 32
 ROWS = 128
 RES = 512
+FAR = (4, 3, 5)
+NEAR = (2, 6, 1, 7)
 
 
 def dot(a, b):
@@ -85,8 +87,8 @@
     pd_h, ag_h, pg_h, wo_h,
     pd_out, ag_out, pg_out, wo_out,
     msa, stretch, shift, wlrt_v, offs, wf, fbias, adj,
-    scaled, inv, nf, nb, np_, wl4t, wrt, lrow, rt,
-    sb, rb, rbf, ls, rs, lmat, lt, rmat, amat, wff, w2, w2t,
+    scaled, inv, nf, nb, np_, wl4t, wrt, rt,
+    sb, rb, rbf, las, la, laf, lbf, lb, lbr, lbrf, lgf, rs, lmat, lt, rmat, amat, wff, w2, w2t,
     gmat, xmat, rgs, rgr, rgo, ryq, ryr, rz, rzr, lacc, lgs, lzr, bsf, bs, br, ng,
     wpart, wsend, wrecv, wzs, wzr, wfin, wall_v, pdb,
     psend, precv, pzs, pzr, pgs, pgr,
@@ -120,6 +122,14 @@
 
     def zs(body):
         for k in (4, 3, 5, 2, 6, 1, 7):
+            body(lax.rem(z + k, NZ))
+
+    def zs_far(body):
+        for k in FAR:
+            body(lax.rem(z + k, NZ))
+
+    def zs_near(body):
+        for k in NEAR:
             body(lax.rem(z + k, NZ))
 
     def xs(body):
@@ -184,12 +194,12 @@
 
     loop(0, 8, norm_rows)
     for r in range(4):
-        for yc in range(4):
-            start = (yc // 2) * 256 + (yc % 2) * 4 + r
-            for h in range(2):
-                np_[pl.ds(r * 128 + yc * 32, 32), pl.ds(h * 128, 128)] = nf[
-                    h, pl.ds(start, 32, stride=8), :
-                ].astype(bf16)
+        for zz in range(NZ):
+            v = [
+                jnp.concatenate([nf[h, pl.ds(yy * 256 + zz * 32 + r, 8, stride=4), :] for h in range(2)], axis=1)
+                for yy in range(2)
+            ]
+            np_[pl.ds(r * 128 + zz * 16, 16), :] = jnp.concatenate(v, axis=0).astype(bf16)
 
     wlrt = wlrt_v[...]
     w_rows = wlrt.astype(f32).T.astype(bf16)
@@ -204,19 +214,21 @@
     left = jnp.zeros((128, 128), f32)
     for r in range(4):
         left = left + dot(np_[pl.ds(r * 128, 128), :], jnp.where(lane_r == r, wl4, 0.0).astype(bf16))
-    lrow[...] = (left + offs4).astype(bf16)
+    left = (left + offs4).astype(bf16).astype(f32) * (1.0 / ROWS)
+    las[...] = left.astype(bf16).reshape(NZ, NM, 128)
     rt[...] = (dot_nt(wlrt[CH:, :], nb[...]) + offs_col[CH:, :]).astype(bf16)
     for mm in range(NM):
-        yc = (mm // 8) * 2 + mm % 2
         xx, cc = (mm % 8) // 2, mm % 2
-        sb[mm, pl.ds(0, 32), :] = lrow[pl.ds(yc * 32, 32), :]
-        sb[mm, pl.ds(32, 16), :] = rt[pl.ds(cc * 16, 16), pl.ds(xx * 128, 128)]
+        sb[mm] = rt[pl.ds(cc * 16, 16), pl.ds(xx * 128, 128)]
 
     pl.semaphore_wait(barrier, NM - 1 + NZ - 1)
 
     first = exchange(planes, plane_dev, m, lambda mm: sb.at[mm], lambda mm: rb.at[mm], rb.at[pl.ds(0, NM - 1)])
     first.start()
     rb[m] = sb[m]
+    zleft = exchange(zs, z_dev, z, lambda zz: las.at[zz], lambda zz: la.at[zz], la.at[pl.ds(0, NZ - 1)])
+    zleft.start()
+    la[z] = las[z]
     adjoint = exchange(xs, x_dev, x, adj_part, own_i, amat.at[pl.ds(0, 12)], adj_r)
     adjoint.start()
     own_adj = pltpu.make_async_copy(adj_part(x), own_i(x), adj_sem)
@@ -230,12 +242,9 @@
 
     first.recv()
 
-    loop(0, NM, lambda k: rbf.__setitem__((pl.ds(pl.multiple_of(k * 48, 48), 48), slice(None)), rb[k].astype(f32)))
-    for zz in range(NZ):
-        for xx in range(NX):
-            ls[zz, :, pl.ds(xx * 128, 128)] = (rbf[pl.ds(zz * 4 + xx, 16, stride=48), :] * (1.0 / ROWS)).astype(bf16)
+    rbf[...] = rb[...].reshape(256, 128).astype(f32)
     for d in range(16):
-        rs[:, pl.ds(d * 128, 128)] = rbf[pl.ds(32 + d, 16, stride=48), :].astype(bf16)
+        rs[:, pl.ds(d * 128, 128)] = rbf[pl.ds(d, 16, stride=16), :].astype(bf16)
 
     def zrows(zz):
         return pl.ds(pl.multiple_of(zz * 16, 16), 16)
@@ -249,20 +258,37 @@
     def r_piece(zz, yy):
         return rmat.at[zrows(zz), quarter(core, yy)]
 
-    zleft = exchange(
-        zs, z_dev, z, lambda zz: ls.at[zz], lambda zz: lmat.at[zrows(zz), :], lmat.at[pl.ds(0, 112), :]
-    )
-    zleft.start()
     rs_own = rs.at[:, pl.ds(pl.multiple_of(y * 1024, 1024), 1024)]
-    zright = exchange(
-        zs, z_dev, z, lambda zz: rs_own, lambda zz: r_piece(zz, y), rmat.at[pl.ds(0, 112), quarter(core, y)], zr_r
-    )
-    zright.start()
-    lmat[zrows(z), :] = ls[z]
+    zfar = exchange(
+        zs_far, z_dev, z, lambda zz: rs_own, lambda zz: r_piece(zz, y), rmat.at[pl.ds(0, 48), quarter(0, 0)], zr_r
+    )
+    znear = exchange(
+        zs_near, z_dev, z, lambda zz: rs, lambda zz: rmat.at[zrows(zz), half(core)], rmat.at[pl.ds(0, 64), half(0)], zr_r
+    )
+    zfar.start()
+    znear.start()
     rmat[zrows(z), half(core)] = rs[...]
 
+    zleft.recv()
+    laf[...] = la[...].reshape(128, 128).astype(f32)
+    for mm in range(0, NM, 2):
+        for cc in range(2):
+            yc, xx = (mm // 8) * 2 + cc, (mm % 8) // 2
+            lbf[pl.ds(yc * 32 + xx * 8, 8), :] = laf[pl.ds(mm + cc, 8, stride=16), :]
+    lb[...] = lbf[...].astype(bf16).reshape(4, 32, 128)
+    lplane = exchange(
+        planes,
+        plane_dev,
+        m,
+        lambda mm: lb.at[(mm // 8) * 2 + lax.rem(mm, 2)],
+        lambda mm: lbr.at[mm],
+        lbr.at[pl.ds(0, NM - 1)],
+    )
+    lplane.start()
+    lbr[m] = lb[y * 2 + core]
+
     yswap = exchange(
-        zs, y_dev, None, lambda zz: r_piece(zz, y), None, rmat.at[pl.ds(0, 112), quarter(core, y)], yf_r
+        zs_far, y_dev, None, lambda zz: r_piece(zz, y), None, rmat.at[pl.ds(0, 48), quarter(0, 0)], yf_r
     )
     swap = exchange(None, core_dev, None, None, None, rmat.at[:, half(other)])
 
@@ -290,9 +316,13 @@
 
     def forward(k):
         zz = lax.rem(z + k, NZ)
-        zright.recv_one(zz)
-        y_copy(zz, y).start()
-        to_core(r_piece(zz, y))
+        if k in FAR:
+            zfar.recv_one(zz)
+            y_copy(zz, y).start()
+            to_core(r_piece(zz, y))
+        else:
+            znear.recv_one(zz)
+            to_core(rmat.at[zrows(zz), half(core)])
 
     def forward_y(k):
         zz = lax.rem(z + k, NZ)
@@ -300,7 +330,8 @@
         to_core(r_piece(zz, 1 - y))
 
     to_core(rmat.at[zrows(z), half(core)])
-    zright.waited = True
+    zfar.waited = True
+    znear.waited = True
     yswap.waited = True
 
     def grad_pair(t):
@@ -322,9 +353,20 @@
         adjoint.recv_one(xx)
         loop(xx * 2, xx * 2 + 2, grad_pair)
 
-    zleft.recv()
+    def left_part(cc, yy):
+        cols = quarter(cc, yy)
+        lacc[...] += dot_nt(rmat[:, cols], gmat[:, cols])
+
+    lplane.recv()
+    lbrf[...] = lbr[...].reshape(512, 128).astype(f32)
+    for zz in range(NZ):
+        for xx in range(NX):
+            lmat[pl.ds(zz * 16, 16), pl.ds(xx * 128, 128)] = lbrf[pl.ds(xx * 8 + zz, 16, stride=32), :].astype(bf16)
     for k in range(4):
         lt[pl.ds(k * 128, 128), :] = lmat[:, pl.ds(k * 128, 128)].astype(f32).T.astype(bf16)
+
+    def columns(ref, yy):
+        return ref.at[:, pl.ds(pl.multiple_of(yy * 1024, 1024), 1024)]
 
     def right_other(yy):
         def part(k):
@@ -333,25 +375,32 @@
 
         loop(0, 2, part)
 
-    def columns(ref, yy):
-        return ref.at[:, pl.ds(pl.multiple_of(yy * 1024, 1024), 1024)]
+    def right_own(yy):
+        def part(k):
+            cols = pl.ds(pl.multiple_of(core * 2048 + yy * 1024 + k * 512, 512), 512)
+            rgo[:, pl.ds(pl.multiple_of(yy * 1024 + k * 512, 512), 512)] = dot(lmat[...], gmat[:, cols])
+
+        loop(0, 2, part)
 
     add = [
-        exchange(lambda body: body(0), core_dev, 0, lambda _: columns(rgs, 1 - y), lambda _: columns(rgr, 1 - y), columns(rgr, 1 - y)),
-        exchange(lambda body: body(0), core_dev, 0, lambda _: columns(rgs, y), lambda _: columns(rgr, y), columns(rgr, y)),
+        exchange(
+            lambda body: body(0),
+            core_dev,
+            0,
+            lambda _, yy=yy: columns(rgs, yy),
+            lambda _, yy=yy: columns(rgr, yy),
+            columns(rgr, yy),
+        )
+        for yy in (1 - y, y)
     ]
     right_other(1 - y)
     add[0].start()
     right_other(y)
     add[1].start()
-
-    def right_own(k):
-        cols = pl.ds(pl.multiple_of(core * 2048 + k * 512, 512), 512)
-        rgo[:, pl.ds(pl.multiple_of(k * 512, 512), 512)] = dot(lmat[...], gmat[:, cols])
-
-    loop(0, 4, right_own)
-    for k in (4, 3, 5, 2):
+    for k in FAR:
         forward(k)
+    right_own(1 - y)
+    right_own(y)
     add[0].recv()
 
     def right_add(k):
@@ -374,13 +423,14 @@
         device_id_type=MESH,
     )
     ry.start()
-    for k in (6, 1, 7):
+    add[1].recv()
+    for k in NEAR:
         forward(k)
-    add[1].recv()
-
-    for k in (4, 3, 5, 2, 6, 1, 7):
+    for k in FAR:
         forward_y(k)
-    swap.recv()
+    lacc[...] = jnp.zeros((128, 512), f32)
+    left_part(core, y)
+    left_part(core, 1 - y)
 
     bright = exchange(
         zs, z_dev, z, lambda zz: rz.at[zrows(zz), :], lambda zz: rzr.at[zz], rzr.at[pl.ds(0, NZ - 1)]
@@ -398,17 +448,18 @@
             rz[zrows(zz), :] = t.astype(bf16)
             bright.start_one(zz)
 
-    lacc[...] = jnp.zeros((128, 512), f32)
-    for n, ks in enumerate([(4, 3), (5, 2), (6, 1), (7, 0)]):
-        lacc[...] += dot_nt(rmat[:, pl.ds(n * 1024, 1024)], gmat[:, pl.ds(n * 1024, 1024)])
-        for k in ks:
-            right_rows(k)
+    for k in (4, 3, 5):
+        right_rows(k)
+    swap.recv()
+    left_part(other, y)
+    left_part(other, 1 - y)
     lgs[...] = (lacc[...] * (1.0 / ROWS)).astype(bf16)
     bleft = exchange(
         zs, z_dev, z, lambda zz: lgs.at[zrows(zz), :], lambda zz: lzr.at[zz], lzr.at[pl.ds(0, NZ - 1)]
     )
     bleft.start()
     lzr[z] = lgs[zrows(z), :]
+
 
     def outer_part(n):
         o = dot(lt[...], rmat[:, pl.ds(pl.multiple_of(n * 256, 256), 256)])
@@ -417,20 +468,10 @@
                 rows = pl.ds(pl.multiple_of((2 * n + e) * 32, 32), 32)
                 xmat[rows, pl.ds(i * 128, 128)] = o[i * 32 : i * 32 + 32, e * 128 : e * 128 + 128].astype(bf16)
 
-    loop(0, 16, outer_part)
-
-    def delta_pair(t):
-        p = dot(w2t[...], xmat[:, pl.ds(pl.multiple_of(t * 256, 256), 256)])
-        pdb[pl.ds(t * 2, 2)] = (p.T + fbias[...]).astype(bf16).reshape(2, 128, 128)
-
-    loop(0, 8, delta_pair)
-
-    def out_part(xx):
-        return pd_out.at[:, pl.ds(pl.multiple_of(xx * 128, 128), 128), :]
-
-    delta = exchange(xs, x_dev, x, lambda xx: pdb.at[pl.ds(xx * 4, 4)], out_part, pd_out.at[:, pl.ds(0, 384), :])
-    delta.start()
-    pd_out[:, pl.ds(pl.multiple_of(x * 128, 128), 128), :] = pdb[pl.ds(x * 4, 4)]
+    for n, ks in enumerate([(2, 6), (1, 7), (0,), ()]):
+        for k in ks:
+            right_rows(k)
+        loop(n * 4, n * 4 + 4, outer_part)
 
     def w_part(n):
         rows = pl.ds(pl.multiple_of(n * 256, 256), 256)
@@ -453,21 +494,35 @@
         bsf[pl.ds(32 + d, 16, stride=48), :] = t
     for zz in range(NZ):
         for xx in range(NX):
-            bsf[pl.ds(zz * 4 + xx, 16, stride=48), :] = lzr[zz, :, pl.ds(xx * 128, 128)].astype(f32)
+            bsf[pl.ds(xx * 8 + zz, 16, stride=48), :] = lzr[zz, :, pl.ds(xx * 128, 128)].astype(f32)
     loop(0, NM, lambda k: bs.__setitem__(k, bsf[pl.ds(pl.multiple_of(k * 48, 48), 48), :].astype(bf16)))
     back = exchange(planes, plane_dev, m, lambda mm: bs.at[mm], lambda mm: br.at[mm], br.at[pl.ds(0, NM - 1)])
     back.start()
     br[m] = bs[m]
 
+    def delta_pair(t):
+        p = dot(w2t[...], xmat[:, pl.ds(pl.multiple_of(t * 256, 256), 256)])
+        pdb[pl.ds(t * 2, 2)] = (p.T + fbias[...]).astype(bf16).reshape(2, 128, 128)
+
+    loop(0, 8, delta_pair)
+
+    def out_part(xx):
+        return pd_out.at[:, pl.ds(pl.multiple_of(xx * 128, 128), 128), :]
+
+    delta = exchange(xs, x_dev, x, lambda xx: pdb.at[pl.ds(xx * 4, 4)], out_part, pd_out.at[:, pl.ds(0, 384), :])
+    delta.start()
+    pd_out[:, pl.ds(pl.multiple_of(x * 128, 128), 128), :] = pdb[pl.ds(x * 4, 4)]
+
     back.recv()
-    lparts = []
-    for yc in range(4):
-        t = None
-        for xx in range(NX):
-            v = br[(yc // 2) * 8 + xx * 2 + yc % 2, pl.ds(0, 32), :].astype(f32)
-            t = v if t is None else t + v
-        lparts.append(t)
-    lg = jnp.concatenate(lparts, axis=0)
+    for yy in range(2):
+        for cc in range(2):
+            t = None
+            for xx in range(NX):
+                v = br[yy * 8 + xx * 2 + cc, pl.ds(0, 32), :].astype(f32)
+                t = v if t is None else t + v
+            for xx in range(NX):
+                lgf[pl.ds(yy * 8 + xx * 2 + cc, 8, stride=16), :] = t[xx * 8 : xx * 8 + 8, :]
+    lg = lgf[...]
     rparts = []
     for cc in range(2):
         for yy in range(2):
@@ -501,10 +556,11 @@
     row_r = lax.broadcasted_iota(jnp.int32, (128, 256), 0) >> 5
     for r in range(4):
         v = dot(lgb, jnp.where(row_r == r, wl4t[...].astype(f32), 0.0).astype(bf16))
-        for yc in range(4):
-            start = (yc // 2) * 256 + (yc % 2) * 4 + r
+        for g in range(16):
             for h in range(2):
-                ng[h, pl.ds(start, 32, stride=8), :] = v[yc * 32 : yc * 32 + 32, h * 128 : h * 128 + 128]
+                ng[h, pl.ds((g % 2) * 256 + (g // 2) * 32 + r, 8, stride=4), :] = v[
+                    g * 8 : g * 8 + 8, h * 128 : h * 128 + 128
+                ]
     nr = dot(rgb.astype(f32).T.astype(bf16), wrt[...])
     ng[0] = ng[0] + nr[:, :128]
     ng[1] = ng[1] + nr[:, 128:]
@@ -594,8 +650,10 @@
         vm((1, 512, 256), bf16), vm((1, 256), f32), vm((1, 256), f32), vm((64, 256), bf16), vm((1, 64), f32),
         vm((1024, 128), bf16), vm((1, 128), f32), vm((4, 512, 128), bf16),
         vm((512, 256), f32), vm((512, 128), f32), vm((2, 512, 128), f32), vm((512, 256), bf16), vm((512, 256), bf16),
-        vm((128, 256), bf16), vm((32, 256), bf16), vm((128, 128), bf16), vm((32, 512), bf16),
-        vm((16, 48, 128), bf16), vm((16, 48, 128), bf16), vm((768, 128), f32), vm((8, 16, 512), bf16),
+        vm((128, 256), bf16), vm((32, 256), bf16), vm((32, 512), bf16),
+        vm((16, 16, 128), bf16), vm((16, 16, 128), bf16), vm((256, 128), f32), vm((8, 16, 128), bf16),
+        vm((8, 16, 128), bf16), vm((128, 128), f32), vm((128, 128), f32), vm((4, 32, 128), bf16), vm((16, 32, 128), bf16),
+        vm((512, 128), f32), vm((128, 128), f32),
         vm((16, 2048), bf16), vm((128, 512), bf16), vm((512, 128), bf16), vm((128, 4096), bf16),
         vm((16, 128, 128), bf16), vm((1024, 128), f32), vm((1024, 128), bf16), vm((128, 1024), bf16),
         vm((512, 4096), bf16), vm((1024, 2048), bf16), vm((128, 2048), bf16), vm((128, 2048), bf16),
@@ -607,7 +665,7 @@
         vm((8, 64, 128), bf16), vm((64, 128), bf16), vm((16, 64, 128), bf16), vm((16, 128, 128), bf16),
         vm((16, 8, 128), f32), vm((16, 8, 128), f32), vm((8, 128), f32), vm((8, 8, 128), f32), vm((8, 128), f32),
         vm((16, 8, 128), f32),
-        sem(8), pltpu.SemaphoreType.DMA, sem(20), sem(20), sem(4), sem(8), sem(8), sem(8),
+        sem(8), pltpu.SemaphoreType.DMA, sem(24), sem(24), sem(4), sem(8), sem(8), sem(8),
     ]
     pd, ag, pg, wo = pl.pallas_call(
         kernel,

time: 75.4 us -> 62.8 us (0.83)
  Pallas kernels: 74.7 us -> 62.1 us
    pallas_call x1, Pallas kernels: 72.4 us -> 59.8 us  [shards(): pl.pallas_call(kernel, out_shape=(jax.ShapeDtypeStruct((4, 512, 128), bf1...]
where the time goes in v3:
time: 62.8 us; the launch traced here: 62.7 us
  Pallas kernels  62.1 us (99%)
  between operations  0.64 us (1%)
    pallas_call x1, Pallas kernels, shards(): pl.pallas_call(kernel, out_shape=(jax.ShapeDtypeStruct((4, 512, 128), bf1...  59.8 us
    pallas_call x1, Pallas kernels, shards(): pl.pallas_call(emit, out_shape=tuple((jax.ShapeDtypeStruct(v.shape, v.dty...  2.26 us

profile of v3, /device:TPU:1, one launch (start us, length us, event | category | flops | bytes accessed | tf_op | source)
XLA Modules:
  0.0 62.7 jit_solution(4872172784711224180)
XLA Ops:
  0.6 59.8 %shard_map.111 = (bf16[4,512,128]{2,1,0:T(8,128)(2,1)}, bf16[1,512,256]{2,1,0:T(8,128)(2,1)}, f32[64,256]{1,0:T(8,128)}, f32[1024,128]{1,0:T(8,128)}) custom-call(bf16[1,512,256]{2,1,0:T(8,128)(2,1)} %msa_h.1, f32[1,256]{1,0:T(1,128)} %bitcast.7, f32[1,256]{1,0:T(1,128)} %bitcast.8, bf16[64,256]{1,0:T(8,128)(2,1)} %bitcast.6, f32[1,64]{1,0:T(1,128)} %bitcast.9, ...), custom_call_target="tpu_custom_call" | custom-call | tf_op jit(solution)/shard_map/pallas_call | solution.py:670
  60.4 2.3 %shard_map.112 = (bf16[4,512,128]{2,1,0:T(8,128)(2,1)}, bf16[1,512,256]{2,1,0:T(8,128)(2,1)}, f32[64,256]{1,0:T(8,128)}, f32[1024,128]{1,0:T(8,128)}) custom-call(bf16[4,512,128]{2,1,0:T(8,128)(2,1)} %get-tuple-element.12.pd, bf16[1,512,256]{2,1,0:T(8,128)(2,1)} %get-tuple-element.13.ag, f32[64,256]{1,0:T(8,128)} %get-tuple-element.14.pg, ...), custom_call_target="tpu_custom_call" | custom-call | tf_op jit(solution)/shard_map/pallas_call | solution.py:694

commit v4 on v3

--- a/solution.py
+++ b/solution.py
@@ -88,8 +88,8 @@
     pd_out, ag_out, pg_out, wo_out,
     msa, stretch, shift, wlrt_v, offs, wf, fbias, adj,
     scaled, inv, nf, nb, np_, wl4t, wrt, rt,
-    sb, rb, rbf, las, la, laf, lbf, lb, lbr, lbrf, lgf, rs, lmat, lt, rmat, amat, wff, w2, w2t,
-    gmat, xmat, rgs, rgr, rgo, ryq, ryr, rz, rzr, lacc, lgs, lzr, bsf, bs, br, ng,
+    sb, rb, rbf, las, la, laf, lbf, lb, lbr, lbrf, rs, lmat, lt, rmat, amat, wff, w2, w2t,
+    gmat, xmat, rgs, rgr, rgo, ryq, ryr, rz, rzf, rzn, rsum, lacc, lgp, lgs, lgr, lzf, lzs, lzr, bsf, bs, br, ng,
     wpart, wsend, wrecv, wzs, wzr, wfin, wall_v, pdb,
     psend, precv, pzs, pzr, pgs, pgr,
     in_sem, adj_sem, ssems, rsems, adj_r, zr_r, yf_r, ry_r,
@@ -260,10 +260,10 @@
 
     rs_own = rs.at[:, pl.ds(pl.multiple_of(y * 1024, 1024), 1024)]
     zfar = exchange(
-        zs_far, z_dev, z, lambda zz: rs_own, lambda zz: r_piece(zz, y), rmat.at[pl.ds(0, 48), quarter(0, 0)], zr_r
+        zs_far, z_dev, z, lambda zz: rs_own, lambda zz: r_piece(zz, y), rmat.at[pl.ds(0, 16 * len(FAR)), quarter(0, 0)], zr_r
     )
     znear = exchange(
-        zs_near, z_dev, z, lambda zz: rs, lambda zz: rmat.at[zrows(zz), half(core)], rmat.at[pl.ds(0, 64), half(0)], zr_r
+        zs_near, z_dev, z, lambda zz: rs, lambda zz: rmat.at[zrows(zz), half(core)], rmat.at[pl.ds(0, 16 * len(NEAR)), half(0)], zr_r
     )
     zfar.start()
     znear.start()
@@ -288,7 +288,7 @@
     lbr[m] = lb[y * 2 + core]
 
     yswap = exchange(
-        zs_far, y_dev, None, lambda zz: r_piece(zz, y), None, rmat.at[pl.ds(0, 48), quarter(0, 0)], yf_r
+        zs_far, y_dev, None, lambda zz: r_piece(zz, y), None, rmat.at[pl.ds(0, 16 * len(FAR)), quarter(0, 0)], yf_r
     )
     swap = exchange(None, core_dev, None, None, None, rmat.at[:, half(other)])
 
@@ -355,7 +355,9 @@
 
     def left_part(cc, yy):
         cols = quarter(cc, yy)
-        lacc[...] += dot_nt(rmat[:, cols], gmat[:, cols])
+        t = dot_nt(rmat[:, cols], gmat[:, cols])
+        for xx in range(NX):
+            lacc[xx] += t[:, xx * 128 : xx * 128 + 128]
 
     lplane.recv()
     lbrf[...] = lbr[...].reshape(512, 128).astype(f32)
@@ -403,17 +405,9 @@
     right_own(y)
     add[0].recv()
 
-    def right_add(k):
-        cols = pl.ds(pl.multiple_of((1 - y) * 1024 + k * 512, 512), 512)
-        ryq[:, pl.ds(pl.multiple_of(k * 512, 512), 512)] = (rgo[:, cols] + rgr[:, cols].astype(f32)).astype(bf16)
-
-    loop(0, 2, right_add)
-
-    def all_z(body):
-        for k in (4, 3, 5, 2, 6, 1, 7, 0):
-            body(lax.rem(z + k, NZ))
-
-    ry = exchange(all_z, y_dev, None, lambda zz: ryq.at[zrows(zz), :], None, ryr, ry_r)
+    ry = exchange(
+        zs_far, y_dev, None, lambda zz: ryq.at[zrows(zz), :], None, ryr.at[pl.ds(0, 16 * len(FAR)), :], ry_r
+    )
     ry.copy = lambda zz, _: pltpu.make_async_remote_copy(
         src_ref=ryq.at[zrows(zz), :],
         dst_ref=ryr.at[zrows(zz), :],
@@ -422,44 +416,52 @@
         device_id={"dap": y_dev(0)},
         device_id_type=MESH,
     )
-    ry.start()
+    theirs = pl.ds(pl.multiple_of((1 - y) * 1024, 1024), 1024)
+    mine = pl.ds(pl.multiple_of(y * 1024, 1024), 1024)
+    for k in FAR:
+        rows = zrows(lax.rem(z + k, NZ))
+        ryq[rows, :] = (rgo[rows, theirs] + rgr[rows, theirs].astype(f32)).astype(bf16)
+        ry.start_one(lax.rem(z + k, NZ))
+    bfar = exchange(
+        zs_far, z_dev, z, lambda zz: rz.at[zrows(zz), mine], lambda zz: rzf.at[zz], rzf.at[pl.ds(0, len(FAR))]
+    )
+    bnear = exchange(
+        zs_near, z_dev, z, lambda zz: rz.at[zrows(zz), :], lambda zz: rzn.at[zz], rzn.at[pl.ds(0, len(NEAR))]
+    )
     add[1].recv()
+    for k in NEAR:
+        rows = zrows(lax.rem(z + k, NZ))
+        rz[rows, :] = (rgo[rows, :] + rgr[rows, :].astype(f32)).astype(bf16)
+        bnear.start_one(lax.rem(z + k, NZ))
     for k in NEAR:
         forward(k)
     for k in FAR:
         forward_y(k)
-    lacc[...] = jnp.zeros((128, 512), f32)
+    lacc[...] = jnp.zeros((NX, 128, 128), f32)
     left_part(core, y)
     left_part(core, 1 - y)
 
-    bright = exchange(
-        zs, z_dev, z, lambda zz: rz.at[zrows(zz), :], lambda zz: rzr.at[zz], rzr.at[pl.ds(0, NZ - 1)]
-    )
-    mine = pl.ds(pl.multiple_of(y * 1024, 1024), 1024)
     ry.waited = True
 
     def right_rows(k):
         zz = lax.rem(z + k, NZ)
+        rows = zrows(zz)
         ry.recv_one(zz)
-        t = rgo[zrows(zz), mine] + rgr[zrows(zz), mine].astype(f32) + ryr[zrows(zz), :].astype(f32)
-        if k == 0:
-            rzr[z] = t.astype(bf16)
-        else:
-            rz[zrows(zz), :] = t.astype(bf16)
-            bright.start_one(zz)
-
-    for k in (4, 3, 5):
+        rz[rows, mine] = (rgo[rows, mine] + rgr[rows, mine].astype(f32) + ryr[rows, :].astype(f32)).astype(bf16)
+        bfar.start_one(zz)
+
+    for k in FAR[:3]:
         right_rows(k)
     swap.recv()
     left_part(other, y)
     left_part(other, 1 - y)
-    lgs[...] = (lacc[...] * (1.0 / ROWS)).astype(bf16)
-    bleft = exchange(
-        zs, z_dev, z, lambda zz: lgs.at[zrows(zz), :], lambda zz: lzr.at[zz], lzr.at[pl.ds(0, NZ - 1)]
-    )
+    for xx in range(NX):
+        for mm in range(NM):
+            lgp[mm, pl.ds(xx * 8, 8), :] = lacc[xx, pl.ds(mm, 8, stride=16), :]
+    lgs[...] = (lgp[...] * (1.0 / ROWS)).astype(bf16)
+    bleft = exchange(planes, plane_dev, m, lambda mm: lgs.at[mm], lambda mm: lgr.at[mm], lgr.at[pl.ds(0, NM - 1)])
     bleft.start()
-    lzr[z] = lgs[zrows(z), :]
-
+    lgr[m] = lgs[m]
 
     def outer_part(n):
         o = dot(lt[...], rmat[:, pl.ds(pl.multiple_of(n * 256, 256), 256)])
@@ -468,10 +470,41 @@
                 rows = pl.ds(pl.multiple_of((2 * n + e) * 32, 32), 32)
                 xmat[rows, pl.ds(i * 128, 128)] = o[i * 32 : i * 32 + 32, e * 128 : e * 128 + 128].astype(bf16)
 
-    for n, ks in enumerate([(2, 6), (1, 7), (0,), ()]):
+    for n, ks in enumerate([FAR[3:4], FAR[4:], (), ()]):
         for k in ks:
             right_rows(k)
         loop(n * 4, n * 4 + 4, outer_part)
+
+    bleft.recv()
+    for yc in range(4):
+        t = None
+        for xx in range(NX):
+            v = lgr[(yc // 2) * 8 + xx * 2 + yc % 2].astype(f32)
+            t = v if t is None else t + v
+        for xx in range(NX):
+            lzf[pl.ds((yc // 2) * 8 + xx * 2 + yc % 2, 8, stride=16), :] = t[xx * 8 : xx * 8 + 8, :]
+    lzs[...] = lzf[...].astype(bf16).reshape(NZ, NM, 128)
+    bzl = exchange(zs, z_dev, z, lambda zz: lzs.at[zz], lambda zz: lzr.at[zz], lzr.at[pl.ds(0, NZ - 1)])
+    bzl.start()
+    lzr[z] = lzs[z]
+
+    bnear.recv()
+    bfar.recv()
+    rows = zrows(z)
+    t = rgo[rows, :] + rgr[rows, :].astype(f32)
+    for k in NEAR:
+        t = t + rzn[lax.rem(z + k, NZ)].astype(f32)
+    rsum[...] = t
+    t = rsum[:, mine]
+    for k in FAR:
+        t = t + rzf[lax.rem(z + k, NZ)].astype(f32)
+    rsum[:, mine] = t
+    for d in range(16):
+        bsf[pl.ds(d, 16, stride=16), :] = rsum[:, pl.ds(d * 128, 128)]
+    bs[...] = bsf[...].astype(bf16).reshape(NM, 16, 128)
+    back = exchange(planes, plane_dev, m, lambda mm: bs.at[mm], lambda mm: br.at[mm], br.at[pl.ds(0, NM - 1)])
+    back.start()
+    br[m] = bs[m]
 
     def w_part(n):
         rows = pl.ds(pl.multiple_of(n * 256, 256), 256)
@@ -484,50 +517,20 @@
     wplane.start()
     wrecv[m] = wsend[m]
 
-    bright.recv()
-    bleft.recv()
-    bsf[...] = jnp.zeros((768, 128), f32)
-    for d in range(8):
-        t = rzr[0, :, pl.ds(d * 128, 128)].astype(f32)
-        for zz in range(1, NZ):
-            t = t + rzr[zz, :, pl.ds(d * 128, 128)].astype(f32)
-        bsf[pl.ds(32 + d, 16, stride=48), :] = t
-    for zz in range(NZ):
-        for xx in range(NX):
-            bsf[pl.ds(xx * 8 + zz, 16, stride=48), :] = lzr[zz, :, pl.ds(xx * 128, 128)].astype(f32)
-    loop(0, NM, lambda k: bs.__setitem__(k, bsf[pl.ds(pl.multiple_of(k * 48, 48), 48), :].astype(bf16)))
-    back = exchange(planes, plane_dev, m, lambda mm: bs.at[mm], lambda mm: br.at[mm], br.at[pl.ds(0, NM - 1)])
-    back.start()
-    br[m] = bs[m]
 
     def delta_pair(t):
         p = dot(w2t[...], xmat[:, pl.ds(pl.multiple_of(t * 256, 256), 256)])
         pdb[pl.ds(t * 2, 2)] = (p.T + fbias[...]).astype(bf16).reshape(2, 128, 128)
 
-    loop(0, 8, delta_pair)
-
-    def out_part(xx):
-        return pd_out.at[:, pl.ds(pl.multiple_of(xx * 128, 128), 128), :]
-
-    delta = exchange(xs, x_dev, x, lambda xx: pdb.at[pl.ds(xx * 4, 4)], out_part, pd_out.at[:, pl.ds(0, 384), :])
-    delta.start()
-    pd_out[:, pl.ds(pl.multiple_of(x * 128, 128), 128), :] = pdb[pl.ds(x * 4, 4)]
+    loop(0, 4, delta_pair)
 
     back.recv()
-    for yy in range(2):
-        for cc in range(2):
-            t = None
-            for xx in range(NX):
-                v = br[yy * 8 + xx * 2 + cc, pl.ds(0, 32), :].astype(f32)
-                t = v if t is None else t + v
-            for xx in range(NX):
-                lgf[pl.ds(yy * 8 + xx * 2 + cc, 8, stride=16), :] = t[xx * 8 : xx * 8 + 8, :]
-    lg = lgf[...]
+    bzl.recv()
+    lg = lzr[...].reshape(128, 128).astype(f32)
     rparts = []
     for cc in range(2):
-        for yy in range(2):
-            row = [br[yy * 8 + xx * 2 + cc, pl.ds(32, 16), :].astype(f32)[:8] for xx in range(NX)]
-            rparts.append(jnp.concatenate(row, axis=1))
+        row = [br[xx * 2 + cc].astype(f32) + br[8 + xx * 2 + cc].astype(f32) for xx in range(NX)]
+        rparts.append(jnp.concatenate(row, axis=1))
     rg = jnp.concatenate(rparts, axis=0)
     lgb = lg.astype(bf16)
     lgt = lgb.astype(f32).T
@@ -544,6 +547,7 @@
     pplane.start()
     precv[m] = psend[m]
 
+    loop(4, 8, delta_pair)
     wplane.recv()
     t = wrecv[0].astype(f32)
     for mm in range(1, NM):
@@ -573,6 +577,14 @@
     pz = exchange(zs, z_dev, z, lambda zz: pzs, lambda zz: pzr.at[zz], pzr.at[pl.ds(0, NZ - 1)])
     pz.start()
     pzr[z] = t
+
+    def out_part(xx):
+        return pd_out.at[:, pl.ds(pl.multiple_of(xx * 128, 128), 128), :]
+
+    delta = exchange(xs, x_dev, x, lambda xx: pdb.at[pl.ds(xx * 4, 4)], out_part, pd_out.at[:, pl.ds(0, 384), :])
+    delta.start()
+    pd_out[:, pl.ds(pl.multiple_of(x * 128, 128), 128), :] = pdb[pl.ds(x * 4, 4)]
+
     def back_rows(k):
         rows = pl.ds(pl.multiple_of(k * 64, 64), 64)
         hid = jnp.concatenate([ng[0, rows, :], ng[1, rows, :]], axis=1) * stretch[...]
@@ -608,13 +620,13 @@
     pall.start()
     pgr[m] = t
 
-    delta.recv()
-    pd_copy = pltpu.make_async_copy(pd_out, pd_h, in_sem.at[1])
-    pd_copy.start()
     wall.recv()
     wo_out[...] = wall_v[...].reshape(1024, 128).astype(f32)
     wo_copy = pltpu.make_async_copy(wo_out, wo_h, in_sem.at[2])
     wo_copy.start()
+    delta.recv()
+    pd_copy = pltpu.make_async_copy(pd_out, pd_h, in_sem.at[1])
+    pd_copy.start()
     pall.recv()
     pt = pgr[...].reshape(2, 64, 128)
     pg_out[:, pl.ds(0, 128)] = pt[0]
@@ -626,16 +638,13 @@
         c.wait()
 
 
-def emit(pd, ag, pg, wo, pd_o, ag_o, pg_o, wo_o, pd_v, ag_v, pg_v, wo_v, sems):
-    parts = [(pd.at[k], pd_v.at[k], pd_o.at[k]) for k in range(4)]
-    parts += [(ag, ag_v, ag_o), (pg, pg_v, pg_o), (wo, wo_v, wo_o)]
-    for k, (src, mid, _) in enumerate(parts):
-        pltpu.make_async_copy(src, mid, sems.at[k]).start()
-    for k, (src, mid, dst) in enumerate(parts):
-        pltpu.make_async_copy(src, mid, sems.at[k]).wait()
-        pltpu.make_async_copy(mid, dst, sems.at[k]).start()
-    for k, (_, mid, dst) in enumerate(parts):
-        pltpu.make_async_copy(mid, dst, sems.at[k]).wait()
+def emit(pd, ag, pg, wo, pd_o, ag_o, pg_o, wo_o, sems):
+    copies = [(pd.at[k], pd_o.at[k]) for k in range(4)] + [(ag, ag_o), (pg, pg_o), (wo, wo_o)]
+    copies = [pltpu.make_async_copy(src, dst, sems.at[k]) for k, (src, dst) in enumerate(copies)]
+    for c in copies:
+        c.start()
+    for c in copies:
+        c.wait()
 
 
 def shards(msa, stretch, shift, wlr, offs, wf, fbias, adj):
@@ -653,14 +662,15 @@
         vm((128, 256), bf16), vm((32, 256), bf16), vm((32, 512), bf16),
         vm((16, 16, 128), bf16), vm((16, 16, 128), bf16), vm((256, 128), f32), vm((8, 16, 128), bf16),
         vm((8, 16, 128), bf16), vm((128, 128), f32), vm((128, 128), f32), vm((4, 32, 128), bf16), vm((16, 32, 128), bf16),
-        vm((512, 128), f32), vm((128, 128), f32),
+        vm((512, 128), f32),
         vm((16, 2048), bf16), vm((128, 512), bf16), vm((512, 128), bf16), vm((128, 4096), bf16),
         vm((16, 128, 128), bf16), vm((1024, 128), f32), vm((1024, 128), bf16), vm((128, 1024), bf16),
         vm((512, 4096), bf16), vm((1024, 2048), bf16), vm((128, 2048), bf16), vm((128, 2048), bf16),
-        vm((128, 2048), f32), vm((128, 1024), bf16), vm((128, 1024), bf16), vm((128, 1024), bf16),
-        vm((8, 16, 1024), bf16), vm((128, 512), f32),
-        vm((128, 512), bf16), vm((8, 16, 512), bf16), vm((768, 128), f32), vm((16, 48, 128), bf16),
-        vm((16, 48, 128), bf16), vm((2, 512, 128), f32),
+        vm((128, 2048), f32), vm((128, 1024), bf16), vm((128, 1024), bf16), vm((128, 2048), bf16),
+        vm((8, 16, 1024), bf16), vm((8, 16, 2048), bf16), vm((16, 2048), f32),
+        vm((4, 128, 128), f32), vm((16, 32, 128), f32), vm((16, 32, 128), bf16), vm((16, 32, 128), bf16),
+        vm((128, 128), f32), vm((8, 16, 128), bf16), vm((8, 16, 128), bf16),
+        vm((256, 128), f32), vm((16, 16, 128), bf16), vm((16, 16, 128), bf16), vm((2, 512, 128), f32),
         vm((1024, 128), f32), vm((16, 64, 128), bf16), vm((16, 64, 128), bf16), vm((64, 128), bf16),
         vm((8, 64, 128), bf16), vm((64, 128), bf16), vm((16, 64, 128), bf16), vm((16, 128, 128), bf16),
         vm((16, 8, 128), f32), vm((16, 8, 128), f32), vm((8, 128), f32), vm((8, 8, 128), f32), vm((8, 128), f32),
@@ -679,25 +689,30 @@
         out_specs=(pl.BlockSpec(memory_space=pltpu.HBM),) * 4,
         scratch_shapes=scratch,
         compiler_params=pltpu.CompilerParams(
-            collective_id=0, has_side_effects=True, vmem_limit_bytes=60 * 1024 * 1024
+            collective_id=0, has_side_effects=True, vmem_limit_bytes=48 * 1024 * 1024
         ),
     )(
-        msa,
-        stretch.reshape(1, 256),
-        shift.reshape(1, 256),
-        wlr.T,
-        offs.reshape(1, 64),
-        wf,
-        fbias.reshape(1, 128),
-        adj,
+        *[
+            pltpu.with_memory_space_constraint(v, pltpu.HBM)
+            for v in (
+                msa,
+                stretch.reshape(1, 256),
+                shift.reshape(1, 256),
+                wlr.T,
+                offs.reshape(1, 64),
+                wf,
+                fbias.reshape(1, 128),
+                adj,
+            )
+        ]
     )
     pd, ag, pg, wo = pl.pallas_call(
         emit,
         out_shape=tuple(jax.ShapeDtypeStruct(v.shape, v.dtype) for v in (pd, ag, pg, wo)),
-        in_specs=[pl.BlockSpec(memory_space=pltpu.HBM)] * 4,
+        in_specs=[pl.BlockSpec(memory_space=pl.ANY)] * 4,
         out_specs=(pl.BlockSpec(memory_space=pltpu.HBM),) * 4,
-        scratch_shapes=[vm((4, 512, 128), bf16), vm((1, 512, 256), bf16), vm((64, 256), f32), vm((1024, 128), f32), sem(7)],
-        compiler_params=pltpu.CompilerParams(vmem_limit_bytes=60 * 1024 * 1024),
+        scratch_shapes=[sem(7)],
+        compiler_params=pltpu.CompilerParams(vmem_limit_bytes=16 * 1024 * 1024),
     )(pd, ag, pg, wo)
     return pd, ag, pg.T, wo
 

time: 62.8 us -> 57.7 us (0.919)
  Pallas kernels: 62.1 us -> 56.9 us
    pallas_call x1, Pallas kernels: 59.8 us -> 55.8 us  [shards(): pl.pallas_call(kernel, out_shape=(jax.ShapeDtypeStruct((4, 512, 128), bf1...]
    pallas_call x1, Pallas kernels: 2.26 us -> 1.14 us  [shards(): pl.pallas_call(emit, out_shape=tuple((jax.ShapeDtypeStruct(v.shape, v.dty...]
where the time goes in v4:
time: 57.7 us; the launch traced here: 57.6 us
  Pallas kernels  56.9 us (99%)
  between operations  0.64 us (1%)
    pallas_call x1, Pallas kernels, shards(): pl.pallas_call(kernel, out_shape=(jax.ShapeDtypeStruct((4, 512, 128), bf1...  55.8 us

profile of v4, /device:TPU:1, one launch (start us, length us, event | category | flops | bytes accessed | tf_op | source)
XLA Modules:
  0.0 57.6 jit_solution(13419436430056255012)
XLA Ops:
  0.6 55.8 %shard_map.111 = (bf16[4,512,128]{2,1,0:T(8,128)(2,1)S(1)}, bf16[1,512,256]{2,1,0:T(8,128)(2,1)S(1)}, f32[64,256]{1,0:T(8,128)S(1)}, f32[1024,128]{1,0:T(8,128)S(1)}) custom-call(bf16[1,512,256]{2,1,0:T(8,128)(2,1)} %msa_h.1, f32[1,256]{1,0:T(1,128)} %bitcast.7, f32[1,256]{1,0:T(1,128)} %bitcast.8, bf16[64,256]{1,0:T(8,128)(2,1)} %bitcast.6, ...), custom_call_target="tpu_custom_call" | custom-call | tf_op jit(solution)/shard_map/pallas_call | solution.py:680
  56.4 1.1 %shard_map.112 = (bf16[4,512,128]{2,1,0:T(8,128)(2,1)}, bf16[1,512,256]{2,1,0:T(8,128)(2,1)}, f32[64,256]{1,0:T(8,128)}, f32[1024,128]{1,0:T(8,128)}) custom-call(bf16[4,512,128]{2,1,0:T(8,128)(2,1)S(1)} %get-tuple-element.12.pd, bf16[1,512,256]{2,1,0:T(8,128)(2,1)S(1)} %get-tuple-element.13.ag, f32[64,256]{1,0:T(8,128)S(1)} %get-tuple-element.14.pg, ...), custom_call_target="tpu_custom_call" | custom-call | tf_op jit(solution)/shard_map/pallas_call | solution.py:709

commit v5 on v4

--- a/solution.py
+++ b/solution.py
@@ -475,6 +475,12 @@
             right_rows(k)
         loop(n * 4, n * 4 + 4, outer_part)
 
+    def w_part(n):
+        rows = pl.ds(pl.multiple_of(n * 256, 256), 256)
+        wpart[rows, :] = dot(xmat[rows, :], amat[...].reshape(2048, 128))
+
+    loop(0, 2, w_part)
+
     bleft.recv()
     for yc in range(4):
         t = None
@@ -506,11 +512,7 @@
     back.start()
     br[m] = bs[m]
 
-    def w_part(n):
-        rows = pl.ds(pl.multiple_of(n * 256, 256), 256)
-        wpart[rows, :] = dot(xmat[rows, :], amat[...].reshape(2048, 128))
-
-    loop(0, 4, w_part)
+    loop(2, 4, w_part)
     for c in range(CH):
         wsend[c // 2, pl.ds((c % 2) * 32, 32), :] = wpart[pl.ds(c, 32, stride=32), :].astype(bf16)
     wplane = exchange(planes, plane_dev, m, lambda mm: wsend.at[mm], lambda mm: wrecv.at[mm], wrecv.at[pl.ds(0, NM - 1)])
@@ -548,6 +550,14 @@
     precv[m] = psend[m]
 
     loop(4, 8, delta_pair)
+
+    def out_part(xx):
+        return pd_out.at[:, pl.ds(pl.multiple_of(xx * 128, 128), 128), :]
+
+    delta = exchange(xs, x_dev, x, lambda xx: pdb.at[pl.ds(xx * 4, 4)], out_part, pd_out.at[:, pl.ds(0, 384), :])
+    delta.start()
+    pd_out[:, pl.ds(pl.multiple_of(x * 128, 128), 128), :] = pdb[pl.ds(x * 4, 4)]
+
     wplane.recv()
     t = wrecv[0].astype(f32)
     for mm in range(1, NM):
@@ -578,12 +588,6 @@
     pz.start()
     pzr[z] = t
 
-    def out_part(xx):
-        return pd_out.at[:, pl.ds(pl.multiple_of(xx * 128, 128), 128), :]
-
-    delta = exchange(xs, x_dev, x, lambda xx: pdb.at[pl.ds(xx * 4, 4)], out_part, pd_out.at[:, pl.ds(0, 384), :])
-    delta.start()
-    pd_out[:, pl.ds(pl.multiple_of(x * 128, 128), 128), :] = pdb[pl.ds(x * 4, 4)]
 
     def back_rows(k):
         rows = pl.ds(pl.multiple_of(k * 64, 64), 64)

time: 57.7 us -> 55.7 us (0.965)
  Pallas kernels: 56.9 us -> 54.9 us
    pallas_call x1, Pallas kernels: 55.8 us -> 53.8 us  [shards(): pl.pallas_call(kernel, out_shape=(jax.ShapeDtypeStruct((4, 512, 128), bf1...]
where the time goes in v5:
time: 55.7 us; the launch traced here: 55.6 us
  Pallas kernels  54.9 us (99%)
  between operations  0.64 us (1%)
    pallas_call x1, Pallas kernels, shards(): pl.pallas_call(kernel, out_shape=(jax.ShapeDtypeStruct((4, 512, 128), bf1...  53.8 us
    pallas_call x1, Pallas kernels, shards(): pl.pallas_call(emit, out_shape=tuple((jax.ShapeDtypeStruct(v.shape, v.dty...  1.14 us

profile of v5, /device:TPU:1, one launch (start us, length us, event | category | flops | bytes accessed | tf_op | source)
XLA Modules:
  0.0 55.6 jit_solution(4663322530059569666)
XLA Ops:
  0.6 53.8 %shard_map.111 = (bf16[4,512,128]{2,1,0:T(8,128)(2,1)S(1)}, bf16[1,512,256]{2,1,0:T(8,128)(2,1)S(1)}, f32[64,256]{1,0:T(8,128)S(1)}, f32[1024,128]{1,0:T(8,128)S(1)}) custom-call(bf16[1,512,256]{2,1,0:T(8,128)(2,1)} %msa_h.1, f32[1,256]{1,0:T(1,128)} %bitcast.7, f32[1,256]{1,0:T(1,128)} %bitcast.8, bf16[64,256]{1,0:T(8,128)(2,1)} %bitcast.6, ...), custom_call_target="tpu_custom_call" | custom-call | tf_op jit(solution)/shard_map/pallas_call | solution.py:684
  54.4 1.1 %shard_map.112 = (bf16[4,512,128]{2,1,0:T(8,128)(2,1)}, bf16[1,512,256]{2,1,0:T(8,128)(2,1)}, f32[64,256]{1,0:T(8,128)}, f32[1024,128]{1,0:T(8,128)}) custom-call(bf16[4,512,128]{2,1,0:T(8,128)(2,1)S(1)} %get-tuple-element.12.pd, bf16[1,512,256]{2,1,0:T(8,128)(2,1)S(1)} %get-tuple-element.13.ag, f32[64,256]{1,0:T(8,128)S(1)} %get-tuple-element.14.pg, ...), custom_call_target="tpu_custom_call" | custom-call | tf_op jit(solution)/shard_map/pallas_call | solution.py:713

commit v6 on v5

--- a/solution.py
+++ b/solution.py
@@ -16,6 +16,7 @@
 CH = 32
 ROWS = 128
 RES = 512
+PLANE_STEPS = [(dy, dx, dc) for dx in (2, 1, 3, 0) for dy in (1, 0) for dc in (1, 0) if dy or dx or dc]
 FAR = (4, 3, 5)
 NEAR = (2, 6, 1, 7)
 
@@ -118,7 +119,8 @@
         return (1 - y) * 64 + z * 8 + x * 2 + core
 
     def planes(body):
-        loop(1, NM, lambda k: body(lax.rem(m + k, NM)))
+        for dy, dx, dc in PLANE_STEPS:
+            body((1 - y if dy else y) * 8 + lax.rem(x + dx, NX) * 2 + (other if dc else core))
 
     def zs(body):
         for k in (4, 3, 5, 2, 6, 1, 7):

time: 55.7 us -> 54.4 us (0.977)
  Pallas kernels: 54.9 us -> 53.7 us
    pallas_call x1, Pallas kernels: 53.8 us -> 52.5 us  [shards(): pl.pallas_call(kernel, out_shape=(jax.ShapeDtypeStruct((4, 512, 128), bf1...]
where the time goes in v6:
time: 54.4 us; the launch traced here: 54.3 us
  Pallas kernels  53.7 us (99%)
  between operations  0.64 us (1%)
    pallas_call x1, Pallas kernels, shards(): pl.pallas_call(kernel, out_shape=(jax.ShapeDtypeStruct((4, 512, 128), bf1...  52.5 us
    pallas_call x1, Pallas kernels, shards(): pl.pallas_call(emit, out_shape=tuple((jax.ShapeDtypeStruct(v.shape, v.dty...  1.14 us

profile of v6, /device:TPU:1, one launch (start us, length us, event | category | flops | bytes accessed | tf_op | source)
XLA Modules:
  0.0 54.3 jit_solution(11378949405019887504)
XLA Ops:
  0.6 52.5 %shard_map.111 = (bf16[4,512,128]{2,1,0:T(8,128)(2,1)S(1)}, bf16[1,512,256]{2,1,0:T(8,128)(2,1)S(1)}, f32[64,256]{1,0:T(8,128)S(1)}, f32[1024,128]{1,0:T(8,128)S(1)}) custom-call(bf16[1,512,256]{2,1,0:T(8,128)(2,1)} %msa_h.1, f32[1,256]{1,0:T(1,128)} %bitcast.7, f32[1,256]{1,0:T(1,128)} %bitcast.8, bf16[64,256]{1,0:T(8,128)(2,1)} %bitcast.6, ...), custom_call_target="tpu_custom_call" | custom-call | tf_op jit(solution)/shard_map/pallas_call | solution.py:686
  53.2 1.1 %shard_map.112 = (bf16[4,512,128]{2,1,0:T(8,128)(2,1)}, bf16[1,512,256]{2,1,0:T(8,128)(2,1)}, f32[64,256]{1,0:T(8,128)}, f32[1024,128]{1,0:T(8,128)}) custom-call(bf16[4,512,128]{2,1,0:T(8,128)(2,1)S(1)} %get-tuple-element.12.pd, bf16[1,512,256]{2,1,0:T(8,128)(2,1)S(1)} %get-tuple-element.13.ag, f32[64,256]{1,0:T(8,128)S(1)} %get-tuple-element.14.pg, ...), custom_call_target="tpu_custom_call" | custom-call | tf_op jit(solution)/shard_map/pallas_call | solution.py:715

commit v7 on v6

--- a/solution.py
+++ b/solution.py
@@ -130,12 +130,15 @@
         for k in FAR:
             body(lax.rem(z + k, NZ))
 
+    def far_step(zz):
+        return lax.rem(zz - z + NZ, NZ) - min(FAR)
+
     def zs_near(body):
         for k in NEAR:
             body(lax.rem(z + k, NZ))
 
     def xs(body):
-        for k in (1, 3, 2):
+        for k in (2, 1, 3):
             body(lax.rem(x + k, NX))
 
     exchanges = []
@@ -309,7 +312,7 @@
             src_ref=r_piece(zz, yy),
             dst_ref=r_piece(zz, yy),
             send_sem=yswap.ssem.at[0],
-            recv_sem=yf_r.at[zz],
+            recv_sem=yf_r.at[far_step(zz)],
             device_id={"dap": y_dev(0)},
             device_id_type=MESH,
         )
@@ -414,7 +417,7 @@
         src_ref=ryq.at[zrows(zz), :],
         dst_ref=ryr.at[zrows(zz), :],
         send_sem=ry.ssem.at[0],
-        recv_sem=ry_r.at[zz],
+        recv_sem=ry_r.at[far_step(zz)],
         device_id={"dap": y_dev(0)},
         device_id_type=MESH,
     )
@@ -681,7 +684,7 @@
         vm((8, 64, 128), bf16), vm((64, 128), bf16), vm((16, 64, 128), bf16), vm((16, 128, 128), bf16),
         vm((16, 8, 128), f32), vm((16, 8, 128), f32), vm((8, 128), f32), vm((8, 8, 128), f32), vm((8, 128), f32),
         vm((16, 8, 128), f32),
-        sem(8), pltpu.SemaphoreType.DMA, sem(24), sem(24), sem(4), sem(8), sem(8), sem(8),
+        sem(8), pltpu.SemaphoreType.DMA, sem(23), sem(23), sem(4), sem(8), sem(3), sem(3),
     ]
     pd, ag, pg, wo = pl.pallas_call(
         kernel,

time: 54.4 us -> 54.2 us (level)
  no operation moved by 1% of the time
where the time goes in v7:
time: 54.2 us; the launch traced here: 54.1 us
  Pallas kernels  53.5 us (99%)
  between operations  0.64 us (1%)
    pallas_call x1, Pallas kernels, shards(): pl.pallas_call(kernel, out_shape=(jax.ShapeDtypeStruct((4, 512, 128), bf1...  52.3 us
    pallas_call x1, Pallas kernels, shards(): pl.pallas_call(emit, out_shape=tuple((jax.ShapeDtypeStruct(v.shape, v.dty...  1.14 us

profile of v7, /device:TPU:1, one launch (start us, length us, event | category | flops | bytes accessed | tf_op | source)
XLA Modules:
  0.0 54.1 jit_solution(5184258232512601881)
XLA Ops:
  0.6 52.3 %shard_map.111 = (bf16[4,512,128]{2,1,0:T(8,128)(2,1)S(1)}, bf16[1,512,256]{2,1,0:T(8,128)(2,1)S(1)}, f32[64,256]{1,0:T(8,128)S(1)}, f32[1024,128]{1,0:T(8,128)S(1)}) custom-call(bf16[1,512,256]{2,1,0:T(8,128)(2,1)} %msa_h.1, f32[1,256]{1,0:T(1,128)} %bitcast.7, f32[1,256]{1,0:T(1,128)} %bitcast.8, bf16[64,256]{1,0:T(8,128)(2,1)} %bitcast.6, ...), custom_call_target="tpu_custom_call" | custom-call | tf_op jit(solution)/shard_map/pallas_call | solution.py:689
  53.0 1.1 %shard_map.112 = (bf16[4,512,128]{2,1,0:T(8,128)(2,1)}, bf16[1,512,256]{2,1,0:T(8,128)(2,1)}, f32[64,256]{1,0:T(8,128)}, f32[1024,128]{1,0:T(8,128)}) custom-call(bf16[4,512,128]{2,1,0:T(8,128)(2,1)S(1)} %get-tuple-element.12.pd, bf16[1,512,256]{2,1,0:T(8,128)(2,1)S(1)} %get-tuple-element.13.ag, f32[64,256]{1,0:T(8,128)S(1)} %get-tuple-element.14.pg, ...), custom_call_target="tpu_custom_call" | custom-call | tf_op jit(solution)/shard_map/pallas_call | solution.py:718
